TPU v7x, 32 devices: a whole 2x2x4 slice. The times are simulated.
32 devices in a mesh: dp: 8 (over z, y), rep: 4 (over x, core).
Axes of the slice: x: 2, y: 2, z: 4, core: 2. Of those that a mesh axis runs over, the one named last changes fastest.
Arguments:
- hop_features: float32 [4, 100, 49152], P(None, None, ('dp', 'rep')), may hold values from -50 to 50
- branch_weight: float32 [4, 100, 512], replicated, may hold values from -0.625 to 0.625
- branch_gain: float32 [2048], replicated, may hold values from 0.5 to 1.5
- branch_bias: float32 [2048], replicated, may hold values from -1.5 to 1.5
- first_slope: float32 [2048], replicated, may hold values from 0.05 to 0.45
- second_slope: float32 [2048], replicated, may hold values from 0.05 to 0.45
- mid_weight: float32 [2048, 512], replicated, may hold values from -0.125 to 0.125
- mid_gain: float32 [512], replicated, may hold values from 0.5 to 1.5
- mid_bias: float32 [512], replicated, may hold values from -1.5 to 1.5
- mid_slope: float32 [512], replicated, may hold values from 0.05 to 0.45
- out_weight: float32 [512, 47], replicated, may hold values from -0.375 to 0.375
- out_bias: float32 [47], replicated, may hold values from -2.5 to 2.5
- labels: int32 [49152], P(('dp', 'rep')), may hold values from 0 to 46
- valid_mask: int32 [49152], P(('dp', 'rep')), may hold values from 0 to 1
Outputs:
- logits: float32 [47, 49152], P(None, ('dp', 'rep'))
- mean_loss: float32 [], replicated
- feature_grad: float32 [4, 100, 49152], P(None, None, ('dp', 'rep'))
- branch_weight_grad: float32 [4, 100, 512], replicated
- branch_gain_grad: float32 [2048], replicated
- branch_bias_grad: float32 [2048], replicated
- first_slope_grad: float32 [2048], replicated
- second_slope_grad: float32 [2048], replicated
- mid_weight_grad: float32 [2048, 512], replicated
- mid_gain_grad: float32 [512], replicated
- mid_bias_grad: float32 [512], replicated
- mid_slope_grad: float32 [512], replicated
- out_weight_grad: float32 [512, 47], replicated
- out_bias_grad: float32 [47], replicated
All inputs are finite; a program needn't handle non-finite values.
Results may differ from a plain program's by a relative error of at most 0.0003.
Values sent between devices are 32-bit elements; how exact they have to be, the bound alone decides.
No kernel may reach another device: no remote copies, remote signals or barrier semaphores. Data moves between devices by JAX's collectives and lax.ppermute only.
A program may use at most 128 MiB of HBM per device.

v0:
```python
import functools

import jax
import jax.numpy as jnp
from jax import lax
from jax.experimental import pallas as pl
from jax.experimental.pallas import tpu as pltpu
from jax.sharding import PartitionSpec as P

epsilon = 1e-05
axes = ("dp", "rep")
exact = lax.Precision.HIGHEST
f32 = jnp.float32
bf16 = jnp.bfloat16
LANES = 128
CHUNK = 256
PIECES = 16
HOP_ROWS = 104
HEAD_ROWS = 56
CLASS_ROWS = 48


def dot(left, right, precision=None):
    return lax.dot_general(
        left, right, (((1,), (0,)), ((), ())), precision=precision, preferred_element_type=f32
    )


def dot_nt(left, right, precision=None):
    return lax.dot_general(
        left, right, (((1,), (1,)), ((), ())), precision=precision, preferred_element_type=f32
    )


def split(values):
    high = values.astype(bf16)
    return high, (values - high.astype(f32)).astype(bf16)


def as_column(row):
    return jnp.broadcast_to(row, (LANES, row.shape[1])).T


def wide(column, width):
    return jnp.concatenate([column] * (width // LANES), axis=1)


def fold(values):
    total = values[:, :LANES]
    for start in range(LANES, values.shape[1], LANES):
        total = total + values[:, start : start + LANES]
    return total


def total_row(partial):
    return jnp.sum(partial.T, axis=0, keepdims=True)


def pad_rows(values, rows):
    return jnp.concatenate(
        [values, jnp.zeros((rows - values.shape[0], values.shape[1]), values.dtype)], axis=0
    )


def weave(products, slabs):
    done = 0
    for j, product in enumerate(products):
        until = (j + 1) * len(slabs) // len(products)
        for slab in slabs[done:until]:
            slab()
        done = until
        product()


def cost(flops=0, bytes_accessed=0):
    return pl.CostEstimate(flops=flops, bytes_accessed=bytes_accessed, transcendentals=0)


def call(kernel, mib, **options):
    return pl.pallas_call(
        kernel, compiler_params=pltpu.CompilerParams(vmem_limit_bytes=mib * 1024 * 1024), **options
    )


class Copies:
    def __init__(self, sems):
        self.sems = sems
        self.used = 0
        self.waiting = []

    def start(self, source, target):
        copy = pltpu.make_async_copy(source, target, self.sems.at[self.used])
        self.used += 1
        copy.start()
        return copy

    def send(self, source, target):
        self.waiting.append(self.start(source, target))

    def finish(self):
        for copy in self.waiting:
            copy.wait()


anywhere = pl.BlockSpec(memory_space=pl.ANY)
vmem = pl.BlockSpec(memory_space=pltpu.VMEM)
smem = pl.BlockSpec(memory_space=pltpu.SMEM)


def aligned(index, step):
    return pl.ds(pl.multiple_of(index * step, step), step)


def stats_kernel(
    x_hbm, w_hbm, mask_ref,
    pay_ref, gram_ref, xcat_hbm, w_out,
    x_scr, w_scr, xcat_ref, row_ref, sems,
):
    copies = Copies(sems)
    hops, feats, _ = x_scr.shape
    x_in, w_in = [], []
    for h in range(hops):
        x_in.append(copies.start(x_hbm.at[:, h, :], x_scr.at[h]))
        w_in.append(copies.start(w_hbm.at[:, h, :], w_scr.at[h]))
    keep = mask_ref[...].reshape(1, -1).astype(f32)
    count = jnp.sum(keep, axis=1, keepdims=True)
    safe = jnp.maximum(count, 1.0)
    row_ref[...] = jnp.zeros_like(row_ref)
    for h in range(hops):
        x_in[h].wait()
        x = x_scr[h]
        mean = jnp.sum(x * keep, axis=1, keepdims=True) / safe
        high, low = split(pad_rows(x - mean, LANES))
        xcat_ref[h, :LANES, :] = high
        xcat_ref[h, LANES:, :] = low
        copies.send(xcat_ref.at[h], xcat_hbm.at[h])
        w_in[h].wait()
        copies.send(w_scr.at[h], w_out.at[h])
        real = jnp.concatenate([high, low], axis=0) * keep.astype(bf16)
        gram = dot_nt(real, real)
        gram = (gram[:LANES, :LANES] + gram[LANES:, LANES:]) + (
            gram[:LANES, LANES:] + gram[LANES:, :LANES]
        )
        gram_ref[h] = gram
        w = pad_rows(w_scr[h], LANES)
        square = jnp.sum(dot(gram, w, exact) * w, axis=0, keepdims=True)
        tiles = w.shape[1] // LANES
        for i in range(tiles):
            row_ref[h * 5 + i : h * 5 + i + 1, :] = square[:, i * LANES : (i + 1) * LANES]
        mean = pad_rows(jnp.broadcast_to(mean, (feats, LANES)), LANES).T
        row_ref[h * 5 + 4 : h * 5 + 5, :] = mean[:1]
        row_ref[h * 5 + 4 : h * 5 + 5, LANES - 1 :] = count
    pay_ref[...] = jnp.broadcast_to(row_ref[...][None], pay_ref.shape)
    copies.finish()


def real_nodes(pay_ref):
    return pay_ref[:, 4, LANES - 1 :]


def feature_shift(pay_ref, h):
    means = pay_ref[:, h * 5 + 4, :]
    counts = means[:, LANES - 1 :]
    total = jnp.sum(counts, axis=0, keepdims=True)
    return means - jnp.sum(counts * means, axis=0, keepdims=True) / total


def prepare_kernel(xcat_hbm, w_ref, w2_hbm, pre_hbm, w2cat_hbm, xcat, w2, pre, w2cat, sems):
    copies = Copies(sems)
    hops, _, width = w_ref.shape
    nodes = xcat.shape[2]
    step = 2 * CHUNK
    quarter = width // 4
    ready = []
    for h in range(hops):
        ready.append(copies.start(xcat_hbm.at[h], xcat.at[h]))
        ready.append(copies.start(w2_hbm.at[h * width : (h + 1) * width, :], w2.at[h]))
    for h in range(hops):
        high, low = split(pad_rows(w_ref[h], LANES).T)
        wcat = jnp.concatenate(
            [jnp.concatenate([high, high], axis=1), jnp.concatenate([low, low], axis=1)], axis=0
        )

        def product(start):
            cols = slice(start, start + step)
            value = dot(wcat, xcat[h, :, cols])
            pre[h, :, cols] = value[:width] + value[width:]

        def turn(i):
            at = i * quarter
            high, low = split(w2[h, at : at + quarter, :].T)
            w2cat[h, :, at : at + quarter] = high
            w2cat[h, :, width + at : width + at + quarter] = low

        ready[2 * h].wait()
        ready[2 * h + 1].wait()
        weave(
            [functools.partial(product, start) for start in range(0, nodes, step)],
            [functools.partial(turn, i) for i in range(4)],
        )
        copies.send(pre.at[h], pre_hbm.at[h * width : (h + 1) * width, :])
        copies.send(w2cat.at[h], w2cat_hbm.at[h])
    copies.finish()


def columns_of(pack):
    rows = pack.shape[0]
    return [jnp.broadcast_to(pack[:, i : i + 1], (rows, LANES)) for i in range(6)]


def forward_kernel(
    code_ref, pay_ref, w_ref, gain_ref, bias_ref, slope1_ref, slope2_ref, mask_ref, pre_hbm, w2cat_hbm,
    mid_ref, stat_ref, inv_ref, colpack_ref, act_hbm,
    pre, w2cat, act, shift_ref, row_ref, sems,
):
    copies = Copies(sems)
    hops, _, width = w_ref.shape
    nodes = mid_ref.shape[1]
    ready = []
    for h in range(hops):
        rows = slice(h * width, (h + 1) * width)
        ready.append((
            copies.start(pre_hbm.at[rows, :], pre.at[h]),
            copies.start(w2cat_hbm.at[h], w2cat.at[h]),
        ))
    counts = real_nodes(pay_ref)
    total = jnp.sum(counts, axis=0, keepdims=True)
    for h in range(hops):
        shift = dot(feature_shift(pay_ref, h), pad_rows(w_ref[h], LANES), exact)
        shift_ref[h] = shift
        squares = rows_of(pay_ref, h * 5, width // LANES)
        square = jnp.sum(squares + counts * shift * shift, axis=0, keepdims=True)
        inverse = lax.rsqrt(square / total + epsilon)
        inv_ref[h] = inverse
        scale = 0.5 * gain_ref[h] * inverse
        rows = [
            scale,
            shift_ref[h, pl.ds(code_ref[0], 1), :] * scale + 0.5 * bias_ref[h],
            0.5 + 0.5 * slope1_ref[h],
            0.5 - 0.5 * slope1_ref[h],
            1.0 + slope2_ref[h],
            1.0 - slope2_ref[h],
        ]
        colpack_ref[h] = pad_rows(jnp.concatenate(rows, axis=0), LANES).T

    def slabs(h):
        rows = 16

        def slab(r):
            rs = slice(r, r + rows)
            columns = columns_of(colpack_ref[h, rs, :])
            scale, shift, p1, q1, p2, q2 = (wide(c, nodes) for c in columns)
            half = pre[h, rs, :] * scale + shift
            half = half * (p1 + q1 * jnp.tanh(half))
            high, low = split(half * (p2 + q2 * jnp.tanh(half)))
            act[h, 0, rs, :] = high
            act[h, 1, rs, :] = low

        return [functools.partial(slab, r) for r in range(0, width, rows)]

    def products(h):
        def product(start):
            cols = slice(start, start + CHUNK)
            high, low = act[h, 0, :, cols], act[h, 1, :, cols]
            w2_high, w2_low = w2cat[h, :, :width], w2cat[h, :, width:]
            value = dot(
                jnp.concatenate([w2_high, w2_high, w2_low], axis=1),
                jnp.concatenate([high, low, high], axis=0),
            )
            mid_ref[:, cols] = value if h == 0 else mid_ref[:, cols] + value

        return [functools.partial(product, start) for start in range(0, nodes, CHUNK)]

    for h in range(hops + 1):
        if h < hops:
            for copy in ready[h]:
                copy.wait()
        weave(products(h - 1) if h else [lambda: None], slabs(h) if h < hops else [])
        if h < hops:
            rows = slice(h * width, (h + 1) * width)
            copies.send(act.at[h, 0], act_hbm.at[0, rows, :])
            copies.send(act.at[h, 1], act_hbm.at[1, rows, :])
    keep = mask_ref[...].reshape(1, -1).astype(f32)
    count = jnp.maximum(jnp.sum(keep, axis=1, keepdims=True), 1.0)
    mid = mid_ref[...]
    average = total_row(fold(mid * keep)) / count
    off = mid - wide(as_column(average), nodes)
    square = total_row(fold(off * off * keep))
    put_rows(row_ref, average, square)
    stat_ref[...] = jnp.broadcast_to(row_ref[...][None], stat_ref.shape)
    copies.finish()


def put_rows(row_ref, *rows):
    at = 0
    for row in rows:
        for start in range(0, row.shape[1], LANES):
            row_ref[at : at + 1, :] = row[:, start : start + LANES]
            at += 1


def rows_of(ref, first, count):
    return jnp.concatenate([ref[:, i, :] for i in range(first, first + count)], axis=1)


def head_kernel(
    pay_ref, stat_ref, gain_ref, bias_ref, slope_ref, ow_ref, ob_ref, label_ref, mask_ref, mid_ref,
    logit_ref, inv_ref, sums_ref, misc_ref, up_ref, norm_ref,
    ow_scr, ob_scr, row_ref, half_ref, tan_ref, acat_ref, col_ref, back_ref, acc_ref, misc_scr,
):
    width, nodes = mid_ref.shape
    classes = ow_ref.shape[0]
    tiles = width // LANES
    counts = real_nodes(pay_ref)
    total = jnp.sum(counts, axis=0, keepdims=True)
    means = rows_of(stat_ref, 0, tiles)
    average = jnp.sum(counts * means, axis=0, keepdims=True) / total
    off = means - average
    square = jnp.sum(rows_of(stat_ref, tiles, tiles) + counts * off * off, axis=0, keepdims=True)
    inverse = lax.rsqrt(square / total + epsilon)
    inv_ref[...] = inverse
    col_ref[0] = as_column(average)
    col_ref[1] = as_column(inverse)
    col_ref[2] = 0.5 * as_column(gain_ref[...])
    col_ref[3] = 0.5 * as_column(bias_ref[...])
    slope = as_column(slope_ref[...])
    col_ref[4] = 0.5 + 0.5 * slope
    col_ref[5] = 0.5 - 0.5 * slope
    ow_scr[...] = jnp.zeros_like(ow_scr)
    ow_scr[:classes, :] = ow_ref[...]
    ow_t = split(ow_scr[:CLASS_ROWS, :])
    ow = split(ow_scr[...].T)
    ob_scr[...] = jnp.zeros_like(ob_scr)
    ob_scr[:, :classes] = ob_ref[...]
    ob_col = wide(as_column(ob_scr[...])[:CLASS_ROWS], nodes)
    rows = 16
    for r in range(0, width, rows):
        rs = slice(r, r + rows)
        mean, inv, gain, bias, p, q = (wide(col_ref[i, rs], nodes) for i in range(6))
        normed = (mid_ref[rs, :] - mean) * inv
        norm_ref[rs, :] = normed
        half = normed * gain + bias
        tangent = jnp.tanh(half)
        half_ref[rs, :] = half
        tan_ref[rs, :] = tangent
        high, low = split(2.0 * half * (p + q * tangent))
        acat_ref[rs, :] = high
        acat_ref[slice(width + r, width + r + rows), :] = low
    high, low = acat_ref[:width, :], acat_ref[width:, :]
    logits = dot(jnp.concatenate([ow_t[0], ow_t[0]], axis=1), acat_ref[...]) + dot(ow_t[1], high)
    logits = logits + ob_col
    logit_ref[...] = logits[:classes]
    keep = mask_ref[...].reshape(1, -1).astype(f32)
    place = lax.broadcasted_iota(jnp.int32, (CLASS_ROWS, nodes), 0)
    logits = jnp.where(place < classes, logits, -3.0e38)
    shifted = logits - jnp.max(logits, axis=0, keepdims=True)
    weights = jnp.exp(shifted)
    norm = jnp.sum(weights, axis=0, keepdims=True)
    onehot = place == label_ref[...].reshape(1, -1)
    picked = jnp.sum(jnp.where(onehot, shifted, 0.0), axis=0, keepdims=True)
    loss = jnp.sum(fold(keep * (jnp.log(norm) - picked)), axis=1, keepdims=True)
    grad = keep * (weights * (1.0 / norm) - jnp.where(onehot, 1.0, 0.0))
    grad_sum = fold(grad)
    grad_high, grad_low = split(pad_rows(grad, LANES))
    gcat = jnp.concatenate([grad_high, grad_low, grad_high], axis=0)
    owcat = jnp.concatenate([ow[0], ow[0], ow[1]], axis=1)

    def back(start):
        back_ref[:, start : start + CHUNK] = dot(owcat, gcat[:, start : start + CHUNK])

    for start in range(0, nodes, CHUNK):
        back(start)
    both = jnp.concatenate([grad_high, grad_low], axis=0)

    def weight_grad():
        value = dot_nt(both, high)
        value = value[:CLASS_ROWS] + value[LANES : LANES + CLASS_ROWS]
        misc_scr[:CLASS_ROWS, :] = value + dot_nt(grad_high[:CLASS_ROWS], low)

    def slab(r):
        rs = slice(r, r + rows)
        p, q = wide(col_ref[4, rs], nodes), wide(col_ref[5, rs], nodes)
        half, tangent, act_grad = half_ref[rs, :], tan_ref[rs, :], back_ref[rs, :]
        away = half * (1.0 - tangent)
        acc_ref[0, rs] = fold(act_grad * away)
        up = act_grad * (p + q * (tangent + away * (1.0 + tangent)))
        up_ref[rs, :] = up
        acc_ref[1, rs] = fold(up)
        acc_ref[2, rs] = fold(up * norm_ref[rs, :])

    slabs = [functools.partial(slab, r) for r in range(0, width, rows)]
    weave([weight_grad, lambda: None], slabs)
    put_rows(row_ref, total_row(acc_ref[1]), total_row(acc_ref[2]))
    sums_ref[...] = jnp.broadcast_to(row_ref[...][None], sums_ref.shape)
    misc_scr[CLASS_ROWS:, :] = jnp.zeros((HEAD_ROWS - CLASS_ROWS, width), f32)
    misc_scr[CLASS_ROWS : CLASS_ROWS + 1, :] = total_row(acc_ref[0])
    misc_scr[CLASS_ROWS + 1 : CLASS_ROWS + 2, :LANES] = total_row(pad_rows(grad_sum, LANES))
    misc_scr[CLASS_ROWS + 2 : CLASS_ROWS + 3, :1] = loss
    for t in range(tiles):
        misc_ref[t] = misc_scr[:, t * LANES : (t + 1) * LANES]


def mid_grad_kernel(
    code_ref, pay_ref, sums_ref, inv_ref, gain_ref, mask_ref, up_ref, norm_ref, act_hbm,
    out_ref, bg_ref, gcat,
    act, sems,
):
    width, nodes = up_ref.shape
    ready = act_in(1, code_ref, Copies(sems), act_hbm, act)
    tiles = width // LANES
    total = jnp.sum(real_nodes(pay_ref), axis=0, keepdims=True)
    bias_sum = jnp.sum(rows_of(sums_ref, 0, tiles), axis=0, keepdims=True)
    gain_sum = jnp.sum(rows_of(sums_ref, tiles, tiles), axis=0, keepdims=True)
    bg_ref[0:1, :] = bias_sum
    bg_ref[1:2, :] = gain_sum
    scale = as_column(gain_ref[...] * inv_ref[...])
    bias_col = as_column(bias_sum / total)
    gain_col = as_column(gain_sum / total)
    keep = mask_ref[...].reshape(1, -1).astype(f32)
    rows = 16
    for r in range(0, width, rows):
        rs = slice(r, r + rows)
        bias, gain = wide(bias_col[rs], nodes), wide(gain_col[rs], nodes)
        grad = up_ref[rs, :] - bias - norm_ref[rs, :] * gain
        high, low = split(keep * (wide(scale[rs], nodes) * grad))
        gcat[rs, :] = high
        gcat[width + r : width + r + rows, :] = low
    mid_product(code_ref, ready, act, gcat, out_ref)


def act_in(half_sel, code_ref, copies, act_hbm, act):
    parts, _, width, _ = act.shape
    rows = width // 2
    ready = []
    for s in range(parts):
        for r in (0, 1):
            block = (s * 2 + (half_sel ^ (code_ref[s] >> 4))) * 2 + r
            ready.append([
                copies.start(act_hbm.at[i, aligned(block, rows)], act.at[s, i, r * rows : (r + 1) * rows])
                for i in (0, 1)
            ])
    return ready


def mid_product(code_ref, ready, act, gcat, out_ref):
    parts, width, mid = out_ref.shape
    rows = width // PIECES
    size = width // 2
    for s in range(parts):
        code = code_ref[s] & (PIECES - 1)
        for r in (0, 1):
            for copy in ready[s * 2 + r]:
                copy.wait()
            here = slice(r * size, (r + 1) * size)
            value = dot_nt(act[s, 0, here, :], gcat[:mid, :])
            value = value + dot_nt(act[s, 0, here, :], gcat[mid:, :])
            value = value + dot_nt(act[s, 1, here, :], gcat[:mid, :])
            for i in range(size // rows):
                place = (r * (size // rows) + i) ^ code
                out_ref[s, aligned(place, rows), :] = value[i * rows : (i + 1) * rows]


def mid_grad_rest_kernel(code_ref, gcat, act_hbm, out_ref, act, sems):
    ready = act_in(0, code_ref, Copies(sems), act_hbm, act)
    mid_product(code_ref, ready, act, gcat, out_ref)


def backward_kernel(
    code_ref, pay_ref, inv_ref, gain_ref, bias_ref, colpack_ref, w_ref, gram_ref, misc_ref,
    g, w2_hbm, pre_hbm, xcat_hbm,
    pack_ref, feat_hbm,
    w2, pre, xcat, feat, col, down, ucat, acc, prod, rows_scr, sems,
):
    copies = Copies(sems)
    hops, feats, width = w_ref.shape
    mid, nodes = g.shape[0] // 2, g.shape[1]
    tiles = mid // LANES
    size = 2 * CHUNK
    chunks = [slice(start, start + size) for start in range(0, nodes, size)]
    count = len(chunks)
    stages = [(h, j) for h in range(hops) for j in range(count)]
    w_in, z_in, x_in = {}, {}, {}
    for h in range(hops):
        own = slice(h * width, (h + 1) * width)
        w_in[h] = copies.start(w2_hbm.at[own, :], w2.at[h])
        for j, c in enumerate(chunks):
            z_in[h, j] = copies.start(pre_hbm.at[own, c], pre.at[h, :, c])
        x_in[h] = copies.start(xcat_hbm.at[h], xcat.at[h])
    devices = pay_ref.shape[0]
    flip = code_ref[1] * (tiles // 2)
    at = hops * HOP_ROWS
    for t in range(tiles):
        pack_ref[t ^ flip, at : at + HEAD_ROWS, :] = misc_ref[t]
    w2cat, wcat = {}, {}

    def columns(h):
        rows = 64
        for r in range(0, width, rows):
            for k, values in enumerate(columns_of(colpack_ref[h, r : r + rows, :])):
                col[h % 2, k, r : r + rows, :] = values
        acc[h % 2] = jnp.zeros(acc.shape[1:], f32)

    def weights(h):
        high, low = split(pad_rows(w_ref[h], LANES) * (gain_ref[h] * inv_ref[h]))
        wcat[h] = (jnp.concatenate([high, low], axis=0), high)
        high, low = split(0.5 * w2[h])
        w2cat[h] = jnp.concatenate([high, high, low], axis=1)

    def part_of(j, part):
        return slice(chunks[j].start + part * CHUNK, chunks[j].start + (part + 1) * CHUNK)

    def down_product(index, part):
        h, j = stages[index]
        cs = part_of(j, part)
        high, low = g[:mid, cs], g[mid:, cs]
        value = dot(w2cat[h], jnp.concatenate([high, low, high], axis=0))
        down[index % 2, :, part * CHUNK : (part + 1) * CHUNK] = value

    def slab(index, r, rows):
        h, j = stages[index]
        two = h % 2
        rs, cs = slice(r, r + rows), chunks[j]
        scale, shift, p1, q1, p2, q2 = (wide(col[two, k, rs], size) for k in range(6))
        half1 = pre[h, rs, cs] * scale + shift
        grad2 = down[index % 2, rs, :]
        tan1 = jnp.tanh(half1)
        half2 = half1 * (p1 + q1 * tan1)
        tan2 = jnp.tanh(half2)
        away2 = half2 * (1.0 - tan2)
        acc[two, 0, rs] += fold(grad2 * away2)
        grad1 = grad2 * (p2 + q2 * (tan2 + away2 * (1.0 + tan2)))
        away1 = half1 * (1.0 - tan1)
        acc[two, 1, rs] += fold(grad1 * away1)
        grad = grad1 * (p1 + q1 * (tan1 + away1 * (1.0 + tan1)))
        acc[two, 2, rs] += fold(grad)
        acc[two, 3, rs] += fold(grad * half1)
        high, low = split(grad)
        ucat[two, rs, cs] = high
        ucat[two, width + r : width + r + rows, cs] = low

    def feature_product(index, part):
        h, j = stages[index]
        cs = part_of(j, part)
        value = dot(wcat[h][0], ucat[h % 2, :width, cs])
        value = value[:LANES] + value[LANES:] + dot(wcat[h][1], ucat[h % 2, width:, cs])
        feat[h, :, cs] = value[:feats]

    def weight_product(h):
        value = dot_nt(xcat[h], ucat[h % 2, :width, :])
        low = dot_nt(xcat[h, :LANES, :], ucat[h % 2, width:, :])
        prod[h % 2] = value[:LANES] + value[LANES:] + low

    def pack(h):
        two = h % 2
        bias_sum = total_row(acc[two, 2])
        shift = feature_shift(pay_ref, h)
        rows_scr[:devices, :] = shift
        rows_scr[devices:, :] = jnp.broadcast_to(real_nodes(pay_ref), shift.shape)
        own_shift = rows_scr[pl.ds(code_ref[0], 1), :]
        own_count = rows_scr[pl.ds(devices + code_ref[0], 1), :]
        column = as_column(own_shift)
        prod[two] = prod[two] + wide(column, mid) * bias_sum
        prod[two, feats : feats + 1, :] = total_row(acc[two, 1])
        prod[two, feats + 1 : feats + 2, :] = 2.0 * total_row(acc[two, 0])
        prod[two, feats + 2 : feats + 3, :] = bias_sum
        prod[two, feats + 3 : feats + 4, :] = (
            2.0 * total_row(acc[two, 3]) - bias_ref[h] * bias_sum
        ) / gain_ref[h]
        for t in range(tiles):
            pack_ref[t ^ flip, h * HOP_ROWS : (h + 1) * HOP_ROWS, :] = prod[
                two, :HOP_ROWS, t * LANES : (t + 1) * LANES
            ]
        gram = gram_ref[h] + column * (own_shift * own_count)
        pack_ref[h ^ flip, at + HEAD_ROWS :, :] = gram[:HOP_ROWS]

    rows = 16
    columns(0)
    w_in[0].wait()
    weights(0)
    for part in (0, 1):
        down_product(0, part)
    for index, (h, j) in enumerate(stages):
        products = []
        z_in[h, j].wait()
        if j + 1 == count:
            x_in[h].wait()
            if h + 1 < hops:
                w_in[h + 1].wait()
                weights(h + 1)
                columns(h + 1)
        if index + 1 < len(stages):
            products += [functools.partial(down_product, index + 1, part) for part in (0, 1)]
        if index >= 1:
            products += [functools.partial(feature_product, index - 1, part) for part in (0, 1)]
        if j == 0 and h >= 1:
            products.append(functools.partial(weight_product, h - 1))
        if j == 1 and h >= 1:
            copies.send(feat.at[h - 1], feat_hbm.at[h - 1])
            pack(h - 1)
        weave(products, [functools.partial(slab, index, r, rows) for r in range(0, width, rows)])
    for part in (0, 1):
        feature_product(len(stages) - 1, part)
    copies.send(feat.at[hops - 1], feat_hbm.at[hops - 1])
    weight_product(hops - 1)
    pack(hops - 1)
    copies.finish()


def finish_kernel(
    code_ref, pay_ref, inv_ref, mine_ref, other_ref, w_ref, gain_ref, mask_ref, bg_ref, xcat_hbm,
    feat_hbm, fgrad_hbm, wgrad_hbm, gain_out, bias_out, slope1_out, slope2_out, mgain_out, mbias_out, mslope_out,
    owg_out, obg_out, loss_out,
    sum_ref, rows_scr, fgrad, wgrad, feat, xcat, sems,
):
    hops, feats, width = w_ref.shape
    tiles = mine_ref.shape[0] * 2
    half = tiles // 2
    flip = code_ref[1]
    copies = Copies(sems)
    ready = []
    for h in range(hops):
        ready.append((copies.start(feat_hbm.at[h], feat.at[h]), copies.start(xcat_hbm.at[h], xcat.at[h])))

    @pl.when(flip == 0)
    def _():
        for t in range(half):
            sum_ref[:, t * LANES : (t + 1) * LANES] = mine_ref[t]
            sum_ref[:, (half + t) * LANES : (half + t + 1) * LANES] = other_ref[t]

    @pl.when(flip != 0)
    def _():
        for t in range(half):
            sum_ref[:, t * LANES : (t + 1) * LANES] = other_ref[t]
            sum_ref[:, (half + t) * LANES : (half + t + 1) * LANES] = mine_ref[t]

    counts = real_nodes(pay_ref)
    total = jnp.sum(counts, axis=0, keepdims=True)
    keep = mask_ref[...].reshape(1, -1).astype(f32)
    at = hops * HOP_ROWS
    for h in range(hops):
        base = h * HOP_ROWS
        w = pad_rows(w_ref[h], LANES)
        inverse = inv_ref[h]
        scale = gain_ref[h] * inverse
        slope1_out[h] = sum_ref[base + feats : base + feats + 1, :]
        slope2_out[h] = sum_ref[base + feats + 1 : base + feats + 2, :]
        bias_sum = sum_ref[base + feats + 2 : base + feats + 3, :]
        gain_sum = sum_ref[base + feats + 3 : base + feats + 4, :]
        bias_out[h] = bias_sum
        gain_out[h] = gain_sum
        gram = sum_ref[at + HEAD_ROWS : at + HEAD_ROWS + HOP_ROWS, h * LANES : (h + 1) * LANES]
        inner = dot(gram, w, exact)[:feats] * (inverse * gain_sum / total)
        wgrad[h] = scale * (sum_ref[base : base + feats, :] - inner)
        copies.send(wgrad.at[h], wgrad_hbm.at[:, h, :])
        shift = feature_shift(pay_ref, h)
        rows_scr[...] = shift
        own_shift = rows_scr[pl.ds(code_ref[0], 1), :]
        mix = dot_nt(w * (scale * inverse * gain_sum / total), w, exact)
        lane = lax.broadcasted_iota(jnp.int32, (1, LANES), 1)
        off = jnp.sum(w * (scale * bias_sum / total), axis=1, keepdims=True)
        off = off + jnp.sum(mix * jnp.where(lane < feats, own_shift, 0.0), axis=1, keepdims=True)
        high, low = split(mix)
        for copy in ready[h]:
            copy.wait()
        mixed = dot(jnp.concatenate([high, high], axis=1), xcat[h]) + dot(low, xcat[h, :LANES])
        fgrad[h] = keep * (feat[h] - (mixed + off)[:feats])
        copies.send(fgrad.at[h], fgrad_hbm.at[:, h, :])
    owg_out[...] = sum_ref[at : at + owg_out.shape[0], :]
    mslope_out[...] = sum_ref[at + CLASS_ROWS : at + CLASS_ROWS + 1, :]
    obg_out[...] = sum_ref[at + CLASS_ROWS + 1 : at + CLASS_ROWS + 2, : obg_out.shape[1]]
    loss_out[...] = sum_ref[at + CLASS_ROWS + 2 : at + CLASS_ROWS + 3, :1] / total
    mbias_out[...] = bg_ref[0:1, :]
    mgain_out[...] = bg_ref[1:2, :]
    copies.finish()


def place_kernel(pieces, code_ref, *refs):
    out_ref, sems = refs[-2:]
    copies = Copies(sems)
    for ref, (s, first, rows) in zip(refs, pieces):
        for i in range(ref.shape[0] // rows):
            block = s * 2 * PIECES + ((first + i) ^ code_ref[s])
            copies.send(ref.at[pl.ds(i * rows, rows)], out_ref.at[aligned(block, rows)])
    copies.finish()


def exchange(values, bit, devices):
    return lax.ppermute(values, axes, [(i, i ^ (1 << bit)) for i in range(devices)])


def exchange_two(a, bit_a, b, bit_b, devices):
    a, b = lax.optimization_barrier((a, b))
    return lax.optimization_barrier((exchange(a, bit_a, devices), exchange(b, bit_b, devices)))


def swap_halves(a, bit_a, b, bit_b, devices):
    size = a.shape[0] // 2
    ra, rb = exchange_two(a[size:], bit_a, b[size:], bit_b, devices)
    return a[:size] + ra, b[:size] + rb


def code_of(me, order):
    code = 0
    for bit in order:
        code = code * 2 + ((me >> bit) & 1)
    return code


def after(values, *others):
    return lax.optimization_barrier((values, *others))[0]


def on_device(
    devices,
    hop_features,
    branch_weight,
    branch_gain,
    branch_bias,
    first_slope,
    second_slope,
    mid_weight,
    mid_gain,
    mid_bias,
    mid_slope,
    out_weight,
    out_bias,
    labels,
    valid_mask,
):
    hops, feats, nodes = hop_features.shape
    width = branch_weight.shape[2]
    mid = mid_weight.shape[1]
    classes = out_weight.shape[1]
    tiles = mid // LANES
    bits = devices.bit_length() - 1
    me = lax.axis_index(axes).astype(jnp.int32)
    rest = tuple(range(5, bits))
    codes = jnp.stack([code_of(me, (0, 1, 2, 3, 4)), code_of(me, (0, 2, 1, 3, 4))])
    place_code = jnp.stack([me, me & 1])
    shape = jax.ShapeDtypeStruct
    by_hop = lambda v: v.reshape(hops, 1, width)
    gain, bias, slope1, slope2 = map(by_hop, (branch_gain, branch_bias, first_slope, second_slope))
    row = lambda v: v.reshape(1, -1)
    gather = functools.partial(
        lax.all_to_all, axis_name=axes, split_axis=0, concat_axis=0, tiled=True
    )
    dma = pltpu.SemaphoreType.DMA
    scratch = lambda dtype, *dims: pltpu.VMEM(dims, dtype)
    mask = valid_mask

    pay, gram, xcat, w = call(
        stats_kernel,
        60,
        in_specs=[anywhere, anywhere, vmem],
        out_specs=[vmem, vmem, anywhere, anywhere],
        out_shape=(
            shape((devices, 24, LANES), f32), shape((hops, LANES, LANES), f32),
            shape((hops, 2 * LANES, nodes), bf16), shape((hops, feats, width), f32),
        ),
        scratch_shapes=[
            scratch(f32, hops, feats, nodes), scratch(f32, hops, feats, width),
            scratch(bf16, hops, 2 * LANES, nodes), scratch(f32, 24, LANES), dma((4 * hops,)),
        ],
        cost_estimate=cost(1_000_000_000, 8_000_000),
        name="first_stats",
    )(jnp.transpose(hop_features, (1, 0, 2)), jnp.transpose(branch_weight, (1, 0, 2)), mask)
    pay = gather(after(pay, codes, place_code))

    pre, w2cat = call(
        prepare_kernel,
        60,
        in_specs=[anywhere, vmem, anywhere],
        out_specs=[anywhere] * 2,
        out_shape=(shape((hops * width, nodes), f32), shape((hops, mid, 2 * width), bf16)),
        scratch_shapes=[
            scratch(bf16, hops, 2 * LANES, nodes), scratch(f32, hops, width, mid),
            scratch(f32, hops, width, nodes), scratch(bf16, hops, mid, 2 * width), dma((4 * hops,)),
        ],
        cost_estimate=cost(4 * 2 * 4 * hops * LANES * width * nodes, 20_000_000),
        name="prepare",
    )(xcat, w, mid_weight)

    mid_pre, stat, first_inv, colpack, act = call(
        forward_kernel,
        45,
        in_specs=[smem] + [vmem] * 7 + [anywhere] * 2,
        out_specs=[vmem] * 4 + [anywhere],
        out_shape=(
            shape((mid, nodes), f32), shape((devices, 8, LANES), f32), shape((hops, 1, width), f32),
            shape((hops, width, LANES), f32), shape((2, hops * width, nodes), bf16),
        ),
        scratch_shapes=[
            scratch(f32, hops, width, nodes), scratch(bf16, hops, mid, 2 * width),
            scratch(bf16, hops, 2, width, nodes), scratch(f32, hops, devices, width),
            scratch(f32, 8, LANES), dma((4 * hops,)),
        ],
        cost_estimate=cost(3 * 2 * hops * width * mid * nodes, 20_000_000),
        name="forward",
    )(place_code, pay, w, gain, bias, slope1, slope2, mask, pre, w2cat)
    stat = gather(stat)

    logits, mid_inv, sums, misc, up, normed = call(
        head_kernel,
        40,
        in_specs=[vmem] * 10,
        out_specs=[vmem] * 6,
        out_shape=(
            shape((classes, nodes), f32), shape((1, mid), f32), shape((devices, 8, LANES), f32),
            shape((tiles, HEAD_ROWS, LANES), f32), shape((mid, nodes), f32), shape((mid, nodes), f32),
        ),
        scratch_shapes=[
            scratch(f32, LANES, mid), scratch(f32, 1, LANES), scratch(f32, 8, LANES),
            scratch(f32, mid, nodes), scratch(f32, mid, nodes), scratch(bf16, 2 * mid, nodes),
            scratch(f32, 6, mid, LANES), scratch(f32, mid, nodes), scratch(f32, 3, mid, LANES),
            scratch(f32, HEAD_ROWS, mid),
        ],
        cost_estimate=cost(2_000_000_000, 10_000_000),
        name="head",
    )(pay, stat, row(mid_gain), row(mid_bias), row(mid_slope), out_weight.T, row(out_bias), labels, mask, mid_pre)
    sums = gather(sums)

    product_cost = cost(2 * 3 * 2 * width * mid * nodes, 10_000_000)
    send, mid_bg, gcat = call(
        mid_grad_kernel,
        36,
        in_specs=[smem] + [vmem] * 7 + [anywhere],
        out_specs=[vmem] * 3,
        out_shape=(
            shape((2, width, mid), f32), shape((2, mid), f32), shape((2 * mid, nodes), bf16),
        ),
        scratch_shapes=[scratch(bf16, 2, 2, width, nodes), dma((8,))],
        cost_estimate=product_cost,
        name="mid_grad_send",
    )(codes, pay, sums, mid_inv, row(mid_gain), mask, up, normed, act)
    came = exchange(send, 0, devices)
    kept = call(
        mid_grad_rest_kernel,
        40,
        in_specs=[smem, vmem, anywhere],
        out_specs=vmem,
        out_shape=shape((2, width, mid), f32),
        scratch_shapes=[scratch(bf16, 2, 2, width, nodes), dma((8,))],
        cost_estimate=product_cost,
        name="mid_grad_keep",
    )(codes, gcat, act)

    pack_rows = hops * HOP_ROWS + HEAD_ROWS + HOP_ROWS

    def backward(gcat):
        return call(
            backward_kernel,
            52,
            in_specs=[smem] + [vmem] * 9 + [anywhere] * 3,
            out_specs=[vmem, anywhere],
            scratch_shapes=[
                scratch(f32, hops, width, mid), scratch(f32, hops, width, nodes),
                scratch(bf16, hops, 2 * LANES, nodes),
                scratch(f32, hops, feats, nodes), scratch(f32, 2, 6, width, LANES),
                scratch(f32, 2, width, 2 * CHUNK), scratch(bf16, 2, 2 * width, nodes),
                scratch(f32, 2, 4, width, LANES), scratch(f32, 2, LANES, mid),
                scratch(f32, 2 * devices, LANES), dma((3 * hops + (hops + 1) * nodes // CHUNK,)),
            ],
            out_shape=(shape((tiles, pack_rows, LANES), f32), shape((hops, feats, nodes), f32)),
            cost_estimate=cost(hops * 2 * 4 * width * mid * nodes, 24_000_000),
            name="backward",
        )(place_code, pay, first_inv, gain, bias, colpack, w, gram, misc, gcat, mid_weight, pre, xcat)

    a, b = kept[0] + came[0], kept[1] + came[1]
    size = a.shape[0] // 2
    send_a, send_b = a[size:], b[size:]
    ra = exchange(send_a, 1, devices)
    rb = exchange(send_b, 2, devices)
    pack, feat = backward(after(gcat, send_a, send_b))
    a, b = a[:size] + after(ra, pack), b[:size] + after(rb, pack)

    half = tiles // 2
    groups = {}
    for i in range(devices):
        groups.setdefault(i & ~14, []).append(i)
    spread = functools.partial(
        lax.all_to_all, axis_name=axes, split_axis=0, concat_axis=0,
        axis_index_groups=list(groups.values()), tiled=True,
    )
    pack = after(pack, a, b)
    pack = pack[:half] + exchange(pack[half:], 0, devices)
    a, b, pack = lax.optimization_barrier((a, b, pack))
    a, b = swap_halves(a, 2, b, 1, devices)
    pack = spread(pack.reshape(8, -1, LANES))
    part = a.shape[0] // 4
    both = jnp.stack([a.reshape(4, part, mid), b.reshape(4, part, mid)], axis=1)
    both = both[:2] + exchange(both[2:], 3, devices)
    pack = pack.sum(axis=0)
    pack, both = lax.optimization_barrier((pack, both))
    came, pack_came = lax.optimization_barrier(
        (exchange(both[1:], 4, devices), exchange(pack, 4, devices))
    )
    both, pack = both[:1] + came, pack + pack_came
    for bit in rest:
        both, pack = both + exchange(both, bit, devices), pack + exchange(pack, bit, devices)
    pack = jnp.broadcast_to(pack[None], (8,) + pack.shape)
    pack, both = lax.optimization_barrier((pack, both))
    pack = spread(pack).reshape(half, pack_rows, LANES)
    both = jnp.concatenate([both, exchange(both, 4, devices)])
    both = jnp.concatenate([both, exchange(both, 3, devices)])
    a, b = both[:, 0].reshape(-1, mid), both[:, 1].reshape(-1, mid)
    ra, rb = exchange_two(a, 2, b, 1, devices)
    a, b = jnp.concatenate([a, ra]), jnp.concatenate([b, rb])
    a, b = lax.optimization_barrier((a, b))
    ra, rb = exchange(a, 1, devices), exchange(b, 2, devices)
    other_a, other_b = exchange(a, 0, devices), exchange(b, 0, devices)
    pack_other = exchange(pack, 0, devices)

    rows_out = [shape((hops, 1, width), f32)] * 4
    rows_mid = [shape((1, mid), f32)] * 3
    (
        feature_grad, branch_weight_grad, branch_gain_grad, branch_bias_grad, first_slope_grad,
        second_slope_grad, mid_gain_grad, mid_bias_grad, mid_slope_grad, out_weight_grad,
        out_bias_grad, mean_loss,
    ) = call(
        finish_kernel,
        60,
        in_specs=[smem] + [vmem] * 8 + [anywhere] * 2,
        out_specs=[anywhere, anywhere] + [vmem] * 10,
        scratch_shapes=[
            scratch(f32, pack_rows, mid), scratch(f32, devices, LANES), scratch(f32, hops, feats, nodes),
            scratch(f32, hops, feats, width), scratch(f32, hops, feats, nodes),
            scratch(bf16, hops, 2 * LANES, nodes), dma((4 * hops,)),
        ],
        out_shape=(
            shape((feats, hops, nodes), f32), shape((feats, hops, width), f32), *rows_out, *rows_mid,
            shape((classes, mid), f32), shape((1, classes), f32), shape((1, 1), f32),
        ),
        cost_estimate=cost(0, 20_000_000),
        name="finish",
    )(place_code, pay, first_inv, pack, pack_other, w, gain, mask, mid_bg, xcat, feat)

    rows = mid_weight.shape[0] // (4 * PIECES)
    eight = PIECES // 2

    def place(pieces, *base):
        values = [value for value, *_ in pieces]
        kinds = [(s, first, rows) for _, s, first in pieces]
        return call(
            functools.partial(place_kernel, kinds),
            16,
            in_specs=[smem] + [vmem] * len(values) + [anywhere] * len(base),
            out_specs=anywhere,
            scratch_shapes=[dma((len(values) * eight,))],
            out_shape=shape(mid_weight.shape, f32),
            input_output_aliases={1 + len(values): 0} if base else {},
            cost_estimate=cost(0, 4_000_000),
            name="place",
        )(codes, *values, *base)

    grad = place(
        [(a, 0, 0), (b, 1, 0), (other_a, 0, PIECES), (after(other_b, mid_bias_grad), 1, PIECES)]
    )
    ra, rb, grad = lax.optimization_barrier((ra, rb, grad))
    other_ra, other_rb = exchange(ra, 0, devices), exchange(rb, 0, devices)
    grad = place([(ra, 0, eight), (rb, 1, eight)], grad)
    mid_weight_grad = place(
        [(other_ra, 0, PIECES + eight), (after(other_rb, grad), 1, PIECES + eight)], grad
    )

    flat = lambda v: v.reshape(-1)
    return (
        logits,
        mean_loss.reshape(()),
        jnp.transpose(feature_grad, (1, 0, 2)),
        jnp.transpose(branch_weight_grad, (1, 0, 2)),
        flat(branch_gain_grad),
        flat(branch_bias_grad),
        flat(first_slope_grad),
        flat(second_slope_grad),
        mid_weight_grad,
        flat(mid_gain_grad),
        flat(mid_bias_grad),
        flat(mid_slope_grad),
        out_weight_grad.T,
        flat(out_bias_grad),
    )


def solution(mesh):
    devices = mesh.shape["dp"] * mesh.shape["rep"]

    def body(*arrays):
        return on_device(devices, *arrays)

    nodes = P(("dp", "rep"))
    return jax.shard_map(
        body,
        mesh=mesh,
        in_specs=(P(None, None, ("dp", "rep")),) + (P(),) * 11 + (nodes, nodes),
        out_specs=(P(None, ("dp", "rep")), P(), P(None, None, ("dp", "rep"))) + (P(),) * 11,
        check_vma=False,
    )
```

profile of v0, /device:TPU:0, one launch (start us, length us, event | category | flops | bytes accessed | tf_op | source)
XLA Modules:
  0.0 210.1 jit_solution(6530139825971848662)
XLA Ops:
  0.7 8.0 %first_stats.1 = (f32[32,24,128]{2,1,0:T(8,128)}, f32[4,128,128]{2,1,0:T(8,128)}, bf16[4,256,1536]{2,1,0:T(8,128)(2,1)}, f32[4,100,512]{2,1,0:T(8,128)}) custom-call(f32[100,4,1536]{2,1,0:T(4,128)} %bitcast.68, f32[100,4,512]{2,1,0:T(4,128)} %bitcast.70, s32[1536]{0:T(1024)} %mask_ref.9), custom_call_target="tpu_custom_call" | custom-call | flops 1000000000 | bytes 8000000 | tf_op jit(solution)/shard_map/first_stats/pallas_call | solution.py:751
  8.8 7.6 %all-to-all-start = ((f32[32,24,128]{2,1,0:T(8,128)}), f32[32,24,128]{2,1,0:T(8,128)S(1)}, u32[]{:S(2)}, u32[]{:S(2)}) async-start(f32[32,24,128]{2,1,0:T(8,128)} %get-tuple-element.78), calls=%async_computation | async-start | bytes 786432 | tf_op jit(solution)/shard_map/all_to_all | solution.py:767
  16.4 9.6 %prepare.1 = (f32[2048,1536]{1,0:T(8,128)}, bf16[4,512,1024]{2,1,0:T(8,128)(2,1)}) custom-call(bf16[4,256,1536]{2,1,0:T(8,128)(2,1)} %get-tuple-element.80.xcat_hbm, f32[4,100,512]{2,1,0:T(8,128)} %get-tuple-element.79.w_ref, f32[2048,512]{1,0:T(8,128)} %w2_hbm.3), custom_call_target="tpu_custom_call" | custom-call | flops 12884901888 | bytes 20000000 | tf_op jit(solution)/shard_map/prepare/pallas_call | solution.py:769
  26.1 3.2 %all-to-all-done.pay_ref = f32[32,24,128]{2,1,0:T(8,128)S(1)} async-done(((f32[32,24,128]{2,1,0:T(8,128)}), f32[32,24,128]{2,1,0:T(8,128)S(1)}, u32[]{:S(2)}, u32[]{:S(2)}) %all-to-all-start) | async-done | bytes 393248 | tf_op jit(solution)/shard_map/all_to_all | solution.py:767
  29.4 20.2 %forward.1 = (f32[512,1536]{1,0:T(8,128)S(1)}, f32[32,8,128]{2,1,0:T(8,128)S(1)}, f32[4,1,512]{2,1,0:T(1,128)S(1)}, f32[4,512,128]{2,1,0:T(8,128)S(1)}, bf16[2,2048,1536]{2,1,0:T(8,128)(2,1)}) custom-call(s32[2]{0:T(128)S(1)} %get-tuple-element.145.code_ref, f32[32,24,128]{2,1,0:T(8,128)S(1)} %all-to-all-done.pay_ref, f32[4,100,512]{2,1,0:T(8,128)S(1)} %copy-done.1, ...), custom_call_target="tpu_custom_call" | custom-call | flops 9663676416 | bytes 20000000 | tf_op jit(solution)/shard_map/forward/pallas_call | solution.py:783
  50.6 10.7 %all_to_all.25.stat_ref = f32[32,8,128]{2,1,0:T(8,128)S(1)} all-to-all(f32[32,8,128]{2,1,0:T(8,128)S(1)} %get-tuple-element.83), channel_id=1, replica_groups=mesh['dp'=8,'rep'=4] {'dp','rep'}, dimensions={0} | all-to-all | bytes 262144 | tf_op jit(solution)/shard_map/all_to_all | solution.py:800
  61.4 4.4 %head.1 = (f32[47,1536]{1,0:T(8,128)}, f32[1,512]{1,0:T(1,128)S(1)}, f32[32,8,128]{2,1,0:T(8,128)S(1)}, f32[4,56,128]{2,1,0:T(8,128)S(1)}, f32[512,1536]{1,0:T(8,128)S(1)}, /*index=5*/f32[512,1536]{1,0:T(8,128)S(1)}) custom-call(f32[32,24,128]{2,1,0:T(8,128)S(1)} %all-to-all-done.pay_ref, f32[32,8,128]{2,1,0:T(8,128)S(1)} %all_to_all.25.stat_ref, ...), custom_call_target="tpu_custom_call" | custom-call | flops 2000000000 | bytes 10000000 | tf_op jit(solution)/shard_map/head/pallas_call | solution.py:802
  65.7 10.0 %all_to_all.26.sums_ref = f32[32,8,128]{2,1,0:T(8,128)S(1)} all-to-all(f32[32,8,128]{2,1,0:T(8,128)S(1)} %get-tuple-element.87), channel_id=1, replica_groups=mesh['dp'=8,'rep'=4] {'dp','rep'}, dimensions={0} | all-to-all | bytes 262144 | tf_op jit(solution)/shard_map/all_to_all | solution.py:820
  75.7 7.9 %mid_grad_send.1 = (f32[2,512,512]{2,1,0:T(8,128)S(1)}, f32[2,512]{1,0:T(2,128)S(1)}, bf16[1024,1536]{1,0:T(8,128)(2,1)S(1)}) custom-call(s32[2]{0:T(128)S(1)} %get-tuple-element.144.code_ref, f32[32,24,128]{2,1,0:T(8,128)S(1)} %all-to-all-done.pay_ref, f32[32,8,128]{2,1,0:T(8,128)S(1)} %all_to_all.26.sums_ref, f32[1,512]{1,0:T(1,128)S(1)} %get-tuple-element.88.inv_ref, ...), custom_call_target="tpu_custom_call" | custom-call | flops 4831838208 | bytes 10000000 | tf_op jit(solution)/shard_map/mid_grad_send/pallas_call | solution.py:823
  84.5 8.0 %mid_grad_keep.1 = f32[2,512,512]{2,1,0:T(8,128)S(1)} custom-call(s32[2]{0:T(128)S(1)} %get-tuple-element.144.code_ref, bf16[1024,1536]{1,0:T(8,128)(2,1)S(1)} %get-tuple-element.97.gcat.g, bf16[2,2048,1536]{2,1,0:T(8,128)(2,1)} %get-tuple-element.91.act_hbm), custom_call_target="tpu_custom_call" | custom-call | flops 4831838208 | bytes 10000000 | tf_op jit(solution)/shard_map/mid_grad_keep/pallas_call | solution.py:836
  94.6 31.4 %backward.1 = (f32[4,576,128]{2,1,0:T(8,128)}, f32[4,100,1536]{2,1,0:T(8,128)}) custom-call(s32[2]{0:T(128)S(1)} %get-tuple-element.145.code_ref, f32[32,24,128]{2,1,0:T(8,128)S(1)} %all-to-all-done.pay_ref, f32[4,1,512]{2,1,0:T(1,128)S(1)} %get-tuple-element.86.inv_ref, f32[4,1,512]{2,1,0:T(1,128)S(1)} %bitcast.47, f32[4,1,512]{2,1,0:T(1,128)S(1)} %bitcast.54, ...), custom_call_target="tpu_custom_call" | custom-call | flops 12884901888 | bytes 24000000 | tf_op jit(solution)/shard_map/backward/pallas_call | solution.py:850
  127.4 2.0 collective-permute-done.3
  133.0 3.5 %all-to-all-start.3 = ((f32[8,144,128]{2,1,0:T(8,128)}), f32[8,144,128]{2,1,0:T(8,128)S(1)}, u32[]{:S(2)}, u32[]{:S(2)}) async-start(f32[8,144,128]{2,1,0:T(8,128)} %bitcast.19), calls=%async_computation.3 | async-start | bytes 1179648 | tf_op jit(solution)/shard_map/all_to_all | solution.py:888
  136.5 2.3 %collective-permute-done.4 = f32[128,512]{1,0:T(8,128)S(1)} collective-permute-done((f32[128,512]{1,0:T(8,128)S(1)}, f32[128,512]{1,0:T(8,128)S(1)}, u32[]{:S(2)}, u32[]{:S(2)}) %collective-permute-start.4) | collective-permute-done | bytes 262176 | tf_op jit(solution)/shard_map/ppermute | solution.py:688
  138.8 3.3 %collective-permute-done.5 = f32[128,512]{1,0:T(8,128)S(1)} collective-permute-done((f32[128,512]{1,0:T(8,128)S(1)}, f32[128,512]{1,0:T(8,128)S(1)}, u32[]{:S(2)}, u32[]{:S(2)}) %collective-permute-start.5) | collective-permute-done | bytes 262176 | tf_op jit(solution)/shard_map/ppermute | solution.py:688
  142.8 8.0 %collective-permute-done.6 = f32[2,2,32,512]{3,2,0,1:T(8,128)S(1)} collective-permute-done((f32[2,2,32,512]{3,2,0,1:T(8,128)S(1)}, f32[2,2,32,512]{3,2,0,1:T(8,128)S(1)}, u32[]{:S(2)}, u32[]{:S(2)}) %collective-permute-start.6) | collective-permute-done | bytes 262176 | tf_op jit(solution)/shard_map/ppermute | solution.py:688
  151.8 2.1 %collective-permute-start.8 = (f32[144,128]{1,0:T(8,128)S(1)}, f32[144,128]{1,0:T(8,128)S(1)}, u32[]{:S(2)}, u32[]{:S(2)}) collective-permute-start(f32[144,128]{1,0:T(8,128)S(1)} %reduce_sum.9), channel_id=1, source_target_pairs={{0,16},{1,17},{2,18},{3,19},{4,20},{5,21},{6,22},{7,23},{8,24},{9,... | collective-permute-start | bytes 221192 | tf_op jit(solution)/shard_map/ppermute | solution.py:688
  153.9 8.0 %collective-permute-done.8 = f32[144,128]{1,0:T(8,128)S(1)} collective-permute-done((f32[144,128]{1,0:T(8,128)S(1)}, f32[144,128]{1,0:T(8,128)S(1)}, u32[]{:S(2)}, u32[]{:S(2)}) %collective-permute-start.8) | collective-permute-done | bytes 73760 | tf_op jit(solution)/shard_map/ppermute | solution.py:688
  162.8 4.4 %all-to-all-start.4 = ((f32[8,144,128]{2,1,0:T(8,128)}), f32[8,144,128]{2,1,0:T(8,128)S(1)}, u32[]{:S(2)}, u32[]{:S(2)}) async-start(f32[8,144,128]{2,1,0:T(8,128)} %broadcast_in_dim.2), calls=%async_computation.4 | async-start | bytes 1179648 | tf_op jit(solution)/shard_map/all_to_all | solution.py:902
  167.2 1.9 collective-permute-done.10
  169.4 11.7 %collective-permute-done.11 = f32[2,2,32,512]{3,2,0,1:T(8,128)S(1)} collective-permute-done((f32[2,2,32,512]{3,2,0,1:T(8,128)S(1)}, f32[2,2,32,512]{3,2,0,1:T(8,128)S(1)}, u32[]{:S(2)}, u32[]{:S(2)}) %collective-permute-start.11) | collective-permute-done | bytes 262176 | tf_op jit(solution)/shard_map/ppermute | solution.py:688
  184.4 3.4 %collective-permute-done.12 = f32[128,512]{1,0:T(8,128)S(1)} collective-permute-done((f32[128,512]{1,0:T(8,128)S(1)}, f32[128,512]{1,0:T(8,128)S(1)}, u32[]{:S(2)}, u32[]{:S(2)}) %collective-permute-start.12) | collective-permute-done | bytes 262176 | tf_op jit(solution)/shard_map/ppermute | solution.py:688
  193.6 9.1 %finish.1 = (f32[100,4,1536]{2,1,0:T(4,128)}, f32[100,4,512]{2,1,0:T(4,128)}, f32[4,1,512]{2,1,0:T(1,128)}, f32[4,1,512]{2,1,0:T(1,128)}, f32[4,1,512]{2,1,0:T(1...) custom-call(s32[2]{0:T(128)} %copy-done.7, ...), custom_call_target="tpu_custom_call" | custom-call | bytes 20000000 | tf_op jit(solution)/shard_map/finish/pallas_call | solution.py:919
  202.7 2.1 %place.3.refs_2_ = f32[2048,512]{1,0:T(8,128)} custom-call(s32[2]{0:T(128)S(1)} %get-tuple-element.144.code_ref, f32[256,512]{1,0:T(8,128)S(1)} %pad_maximum_fusion.refs_0_, f32[256,512]{1,0:T(8,128)S(1)} %pad_maximum_fusion.1.refs_1_, f32[256,512]{1,0:T(8,128)S(1)} %collective-permute-done.16.refs_2_, f32[256,512]{1,0:T(8,128)S(1)} %collective-permute-done.17.refs_3_), custom_call_target="tpu_custom_call" | custom-call | bytes 4000000 | tf_op jit(solution)/shard_map/place/pallas_call | solution.py:943
  (105 shorter events, 25.9 us)
Async XLA Ops:
  8.8 85.8 %copy-start.7 = (s32[2]{0:T(128)}, s32[2]{0:T(128)S(1)}, u32[]{:S(2)}) copy-start(s32[2]{0:T(128)S(1)} %get-tuple-element.145.code_ref) | copy-start | bytes 28
  8.8 20.5 %all-to-all-start = ((f32[32,24,128]{2,1,0:T(8,128)}), f32[32,24,128]{2,1,0:T(8,128)S(1)}, u32[]{:S(2)}, u32[]{:S(2)}) async-start(f32[32,24,128]{2,1,0:T(8,128)} %get-tuple-element.78), calls=%async_computation | async-start | bytes 786432 | tf_op jit(solution)/shard_map/all_to_all | solution.py:767
  84.3 8.2 %collective-permute-start = (f32[2,512,512]{2,1,0:T(8,128)S(1)}, f32[2,512,512]{2,1,0:T(8,128)S(1)}, u32[]{:S(2)}, u32[]{:S(2)}) collective-permute-start(f32[2,512,512]{2,1,0:T(8,128)S(1)} %get-tuple-element.93), channel_id=1, source_target_pairs={{0,1},{1,0},{2,3},{3,2},{4,5},{5,4},{6,7},{7,6},{8,9},{9,8},{10,11... | collective-permute-start | bytes 6291464 | tf_op jit(solution)/shard_map/ppermute | solution.py:688
  93.1 33.0 %collective-permute-start.1 = (f32[256,512]{1,0:T(8,128)S(1)}, f32[256,512]{1,0:T(8,128)S(1)}, u32[]{:S(2)}, u32[]{:S(2)}) collective-permute-start(f32[256,512]{1,0:T(8,128)S(1)} %slice_bitcast_fusion.2), channel_id=1, source_target_pairs={{0,2},{1,3},{2,0},{3,1},{4,6},{5,7},{6,4},{7,5},{8,10},{9,11},{10,... | collective-permute-start | bytes 1572872 | tf_op jit(solution)/shard_map/ppermute | solution.py:688
  93.6 32.6 %collective-permute-start.2 = (f32[256,512]{1,0:T(8,128)S(1)}, f32[256,512]{1,0:T(8,128)S(1)}, u32[]{:S(2)}, u32[]{:S(2)}) collective-permute-start(f32[256,512]{1,0:T(8,128)S(1)} %slice_bitcast_fusion.1), channel_id=1, source_target_pairs={{0,4},{1,5},{2,6},{3,7},{4,0},{5,1},{6,2},{7,3},{8,12},{9,13},{10,... | collective-permute-start | bytes 1572872 | tf_op jit(solution)/shard_map/ppermute | solution.py:688
  127.3 2.1 collective-permute-start.3
  130.3 8.4 %collective-permute-start.4 = (f32[128,512]{1,0:T(8,128)S(1)}, f32[128,512]{1,0:T(8,128)S(1)}, u32[]{:S(2)}, u32[]{:S(2)}) collective-permute-start(f32[128,512]{1,0:T(8,128)S(1)} %slice.87), channel_id=1, source_target_pairs={{0,4},{1,5},{2,6},{3,7},{4,0},{5,1},{6,2},{7,3},{8,12},{9,13},{10,... | collective-permute-start | bytes 786440 | tf_op jit(solution)/shard_map/ppermute | solution.py:688
  131.4 10.6 %collective-permute-start.5 = (f32[128,512]{1,0:T(8,128)S(1)}, f32[128,512]{1,0:T(8,128)S(1)}, u32[]{:S(2)}, u32[]{:S(2)}) collective-permute-start(f32[128,512]{1,0:T(8,128)S(1)} %slice.88), channel_id=1, source_target_pairs={{0,2},{1,3},{2,0},{3,1},{4,6},{5,7},{6,4},{7,5},{8,10},{9,11},{10,... | collective-permute-start | bytes 786440 | tf_op jit(solution)/shard_map/ppermute | solution.py:688
  133.0 17.9 %all-to-all-start.3 = ((f32[8,144,128]{2,1,0:T(8,128)}), f32[8,144,128]{2,1,0:T(8,128)S(1)}, u32[]{:S(2)}, u32[]{:S(2)}) async-start(f32[8,144,128]{2,1,0:T(8,128)} %bitcast.19), calls=%async_computation.3 | async-start | bytes 1179648 | tf_op jit(solution)/shard_map/all_to_all | solution.py:888
  142.1 8.6 %collective-permute-start.6 = (f32[2,2,32,512]{3,2,0,1:T(8,128)S(1)}, f32[2,2,32,512]{3,2,0,1:T(8,128)S(1)}, u32[]{:S(2)}, u32[]{:S(2)}) collective-permute-start(f32[2,2,32,512]{3,2,0,1:T(8,128)S(1)} %pad_maximum_fusion.2), channel_id=1, source_target_pairs={{0,8},{1,9},{2,10},{3,11},{4,12},{5,13},{6,14},{7,15},{8,0},{9,1},... | collective-permute-start | bytes 786440 | tf_op jit(solution)/shard_map/ppermute | solution.py:688
  150.9 11.0 %collective-permute-start.7 = (f32[1,2,32,512]{3,2,0,1:T(8,128)S(1)}, f32[1,2,32,512]{3,2,0,1:T(8,128)S(1)}, u32[]{:S(2)}, u32[]{:S(2)}) collective-permute-start(f32[1,2,32,512]{3,2,0,1:T(8,128)S(1)} %slice.92), channel_id=1, source_target_pairs={{0,16},{1,17},{2,18},{3,19},{4,20},{5,21},{6,22},{7,23},{8,24},{9,... | collective-permute-start | bytes 393224 | tf_op jit(solution)/shard_map/ppermute | solution.py:688
  151.8 10.1 %collective-permute-start.8 = (f32[144,128]{1,0:T(8,128)S(1)}, f32[144,128]{1,0:T(8,128)S(1)}, u32[]{:S(2)}, u32[]{:S(2)}) collective-permute-start(f32[144,128]{1,0:T(8,128)S(1)} %reduce_sum.9), channel_id=1, source_target_pairs={{0,16},{1,17},{2,18},{3,19},{4,20},{5,21},{6,22},{7,23},{8,24},{9,... | collective-permute-start | bytes 221192 | tf_op jit(solution)/shard_map/ppermute | solution.py:688
  162.8 6.3 %collective-permute-start.10 = (f32[1,2,32,512]{3,2,0,1:T(8,128)S(1)}, f32[1,2,32,512]{3,2,0,1:T(8,128)S(1)}, u32[]{:S(2)}, u32[]{:S(2)}) collective-permute-start(f32[1,2,32,512]{3,2,0,1:T(8,128)S(1)} %slice_add_fusion.5), channel_id=1, source_target_pairs={{0,16},{1,17},{2,18},{3,19},{4,20},{5,21},{6,22},{7,23},{8,24},{9,... | collective-permute-start | bytes 393224 | tf_op jit(solution)/shard_map/ppermute | solution.py:688
  162.8 26.5 %all-to-all-start.4 = ((f32[8,144,128]{2,1,0:T(8,128)}), f32[8,144,128]{2,1,0:T(8,128)S(1)}, u32[]{:S(2)}, u32[]{:S(2)}) async-start(f32[8,144,128]{2,1,0:T(8,128)} %broadcast_in_dim.2), calls=%async_computation.4 | async-start | bytes 1179648 | tf_op jit(solution)/shard_map/all_to_all | solution.py:902
  169.1 12.0 %collective-permute-start.11 = (f32[2,2,32,512]{3,2,0,1:T(8,128)S(1)}, f32[2,2,32,512]{3,2,0,1:T(8,128)S(1)}, u32[]{:S(2)}, u32[]{:S(2)}) collective-permute-start(f32[2,2,32,512]{3,2,0,1:T(8,128)S(1)} %pad_maximum_fusion.3), channel_id=1, source_target_pairs={{0,8},{1,9},{2,10},{3,11},{4,12},{5,13},{6,14},{7,15},{8,0},{9,1},... | collective-permute-start | bytes 786440 | tf_op jit(solution)/shard_map/ppermute | solution.py:688
  181.1 6.6 %collective-permute-start.12 = (f32[128,512]{1,0:T(8,128)S(1)}, f32[128,512]{1,0:T(8,128)S(1)}, u32[]{:S(2)}, u32[]{:S(2)}) collective-permute-start(f32[128,512]{1,0:T(8,128)S(1)} %bitcast.66), channel_id=1, source_target_pairs={{0,4},{1,5},{2,6},{3,7},{4,0},{5,1},{6,2},{7,3},{8,12},{9,13},{10,... | collective-permute-start | bytes 786440 | tf_op jit(solution)/shard_map/ppermute | solution.py:688
  182.9 6.4 %collective-permute-start.13 = (f32[128,512]{1,0:T(8,128)S(1)}, f32[128,512]{1,0:T(8,128)S(1)}, u32[]{:S(2)}, u32[]{:S(2)}) collective-permute-start(f32[128,512]{1,0:T(8,128)S(1)} %bitcast.64), channel_id=1, source_target_pairs={{0,2},{1,3},{2,0},{3,1},{4,6},{5,7},{6,4},{7,5},{8,10},{9,11},{10,... | collective-permute-start | bytes 786440 | tf_op jit(solution)/shard_map/ppermute | solution.py:688
  189.3 3.4 %collective-permute-start.9 = (f32[2,576,128]{2,1,0:T(8,128)S(1)}, f32[2,576,128]{2,1,0:T(8,128)S(1)}, u32[]{:S(2)}, u32[]{:S(2)}) collective-permute-start(f32[2,576,128]{2,1,0:T(8,128)S(1)} %bitcast.58), channel_id=1, source_target_pairs={{0,1},{1,0},{2,3},{3,2},{4,5},{5,4},{6,7},{7,6},{8,9},{9,8},{10,11... | collective-permute-start | bytes 1769480 | tf_op jit(solution)/shard_map/ppermute | solution.py:688
  189.5 13.2 %collective-permute-start.17 = (f32[256,512]{1,0:T(8,128)S(1)}, f32[256,512]{1,0:T(8,128)S(1)}, u32[]{:S(2)}, u32[]{:S(2)}) collective-permute-start(f32[256,512]{1,0:T(8,128)S(1)} %pad_maximum_fusion.1.refs_1_), channel_id=1, source_target_pairs={{0,1},{1,0},{2,3},{3,2},{4,5},{5,4},{6,7},{7,6},{8,9},{9,8},{10,11... | collective-permute-start | bytes 1572872 | tf_op jit(solution)/shard_map/ppermute | solution.py:688
  190.0 12.7 %collective-permute-start.16 = (f32[256,512]{1,0:T(8,128)S(1)}, f32[256,512]{1,0:T(8,128)S(1)}, u32[]{:S(2)}, u32[]{:S(2)}) collective-permute-start(f32[256,512]{1,0:T(8,128)S(1)} %pad_maximum_fusion.refs_0_), channel_id=1, source_target_pairs={{0,1},{1,0},{2,3},{3,2},{4,5},{5,4},{6,7},{7,6},{8,9},{9,8},{10,11... | collective-permute-start | bytes 1572872 | tf_op jit(solution)/shard_map/ppermute | solution.py:688
  190.1 14.7 %collective-permute-start.14 = (f32[256,512]{1,0:T(8,128)S(1)}, f32[256,512]{1,0:T(8,128)S(1)}, u32[]{:S(2)}, u32[]{:S(2)}) collective-permute-start(f32[256,512]{1,0:T(8,128)S(1)} %pad_maximum_fusion.refs_0_), channel_id=1, source_target_pairs={{0,2},{1,3},{2,0},{3,1},{4,6},{5,7},{6,4},{7,5},{8,10},{9,11},{10,... | collective-permute-start | bytes 1572872 | tf_op jit(solution)/shard_map/ppermute | solution.py:688
  191.6 14.0 %collective-permute-start.15 = (f32[256,512]{1,0:T(8,128)S(1)}, f32[256,512]{1,0:T(8,128)S(1)}, u32[]{:S(2)}, u32[]{:S(2)}) collective-permute-start(f32[256,512]{1,0:T(8,128)S(1)} %pad_maximum_fusion.1.refs_1_), channel_id=1, source_target_pairs={{0,4},{1,5},{2,6},{3,7},{4,0},{5,1},{6,2},{7,3},{8,12},{9,13},{10,... | collective-permute-start | bytes 1572872 | tf_op jit(solution)/shard_map/ppermute | solution.py:688
  205.6 2.2 %collective-permute-start.19 = (f32[256,512]{1,0:T(8,128)S(1)}, f32[256,512]{1,0:T(8,128)S(1)}, u32[]{:S(2)}, u32[]{:S(2)}) collective-permute-start(f32[256,512]{1,0:T(8,128)S(1)} %collective-permute-done.15.refs_1_), channel_id=1, source_target_pairs={{0,1},{1,0},{2,3},{3,2},{4,5},{5,4},{6,7},{7,6},{8,9},{9,8},{10,11... | collective-permute-start | bytes 1572872 | tf_op jit(solution)/shard_map/ppermute | solution.py:688
  205.6 2.7 %collective-permute-start.18 = (f32[256,512]{1,0:T(8,128)S(1)}, f32[256,512]{1,0:T(8,128)S(1)}, u32[]{:S(2)}, u32[]{:S(2)}) collective-permute-start(f32[256,512]{1,0:T(8,128)S(1)} %collective-permute-done.14.refs_0_), channel_id=1, source_target_pairs={{0,1},{1,0},{2,3},{3,2},{4,5},{5,4},{6,7},{7,6},{8,9},{9,8},{10,11... | collective-permute-start | bytes 1572872 | tf_op jit(solution)/shard_map/ppermute | solution.py:688
  (21 other events, 396.8 us)
where the time goes:
time: 214 us; the launch traced here: 210 us
  Pallas kernels  104 us (49%)
  waiting for transfers between devices  46.4 us (22%)
  starting transfers between devices  30.9 us (14%)
  blocking collectives  20.7 us (10%)
  local copies, waits for them, and re-layouts  4.71 us (2%)
    ppermute x20, waiting for transfers between devices, exchange(): lax.ppermute(values, axes, [(i, i ^ 1 << bit) for i in range(devices)])  43.2 us
    pallas_call x1, Pallas kernels, backward(): call(backward_kernel, 52, in_specs=[smem] + [vmem] * 9 + [anywhere] * 3,...  31.4 us
    pallas_call x1, Pallas kernels, on_device(): call(forward_kernel, 45, in_specs=[smem] + [vmem] * 7 + [anywhere] * 2, o...  20.2 us
    ppermute x20, starting transfers between devices, exchange(): lax.ppermute(values, axes, [(i, i ^ 1 << bit) for i in range(devices)])  15.3 us
    all_to_all x1, blocking collectives, on_device(): stat = gather(stat)  10.7 us
    all_to_all x1, blocking collectives, on_device(): sums = gather(sums)  10 us
    pallas_call x1, Pallas kernels, on_device(): call(prepare_kernel, 60, in_specs=[anywhere, vmem, anywhere], out_specs=[...  9.63 us
    pallas_call x1, Pallas kernels, on_device(): call(finish_kernel, 60, in_specs=[smem] + [vmem] * 8 + [anywhere] * 2, ou...  9.13 us
  transfers between devices with their start and end apart: 23, of which 12 were waited for; matrix products, arithmetic and copies ran while one was open for 0% of the time, Pallas kernels for 29%

commit v1 on v0

--- a/solution.py
+++ b/solution.py
@@ -126,40 +126,43 @@
     count = jnp.sum(keep, axis=1, keepdims=True)
     safe = jnp.maximum(count, 1.0)
     row_ref[...] = jnp.zeros_like(row_ref)
+    means, grams = [], []
+    place = lax.broadcasted_iota(jnp.int32, (LANES, x_scr.shape[2]), 0)
     for h in range(hops):
         x_in[h].wait()
         x = x_scr[h]
-        mean = jnp.sum(x * keep, axis=1, keepdims=True) / safe
-        high, low = split(pad_rows(x - mean, LANES))
+        means.append(jnp.sum(x * keep, axis=1, keepdims=True) / safe)
+        high, low = split(jnp.where(place == feats, 1.0, pad_rows(x - means[h], LANES)))
         xcat_ref[h, :LANES, :] = high
         xcat_ref[h, LANES:, :] = low
         copies.send(xcat_ref.at[h], xcat_hbm.at[h])
+    for h in range(hops):
+        real = xcat_ref[h] * keep.astype(bf16)
+        gram = dot_nt(real, real)
+        grams.append(
+            (gram[:LANES, :LANES] + gram[LANES:, LANES:]) + (gram[:LANES, LANES:] + gram[LANES:, :LANES])
+        )
+        gram_ref[h] = grams[h]
+    for h in range(hops):
         w_in[h].wait()
         copies.send(w_scr.at[h], w_out.at[h])
-        real = jnp.concatenate([high, low], axis=0) * keep.astype(bf16)
-        gram = dot_nt(real, real)
-        gram = (gram[:LANES, :LANES] + gram[LANES:, LANES:]) + (
-            gram[:LANES, LANES:] + gram[LANES:, :LANES]
-        )
-        gram_ref[h] = gram
+    for h in range(hops):
         w = pad_rows(w_scr[h], LANES)
-        square = jnp.sum(dot(gram, w, exact) * w, axis=0, keepdims=True)
-        tiles = w.shape[1] // LANES
-        for i in range(tiles):
-            row_ref[h * 5 + i : h * 5 + i + 1, :] = square[:, i * LANES : (i + 1) * LANES]
-        mean = pad_rows(jnp.broadcast_to(mean, (feats, LANES)), LANES).T
-        row_ref[h * 5 + 4 : h * 5 + 5, :] = mean[:1]
-        row_ref[h * 5 + 4 : h * 5 + 5, LANES - 1 :] = count
+        width = w.shape[1]
+        row_ref[h : h + 1, :width] = jnp.sum(dot(grams[h], w, exact) * w, axis=0, keepdims=True)
+        mean = pad_rows(jnp.broadcast_to(means[h], (feats, LANES)), LANES).T
+        row_ref[h : h + 1, width:] = mean[:1]
+        row_ref[h : h + 1, width + LANES - 1 :] = count
     pay_ref[...] = jnp.broadcast_to(row_ref[...][None], pay_ref.shape)
     copies.finish()
 
 
 def real_nodes(pay_ref):
-    return pay_ref[:, 4, LANES - 1 :]
+    return pay_ref[:, 0, pay_ref.shape[2] - 1 :]
 
 
 def feature_shift(pay_ref, h):
-    means = pay_ref[:, h * 5 + 4, :]
+    means = pay_ref[:, h, pay_ref.shape[2] - LANES :]
     counts = means[:, LANES - 1 :]
     total = jnp.sum(counts, axis=0, keepdims=True)
     return means - jnp.sum(counts * means, axis=0, keepdims=True) / total
@@ -228,7 +231,7 @@
     for h in range(hops):
         shift = dot(feature_shift(pay_ref, h), pad_rows(w_ref[h], LANES), exact)
         shift_ref[h] = shift
-        squares = rows_of(pay_ref, h * 5, width // LANES)
+        squares = pay_ref[:, h, :width]
         square = jnp.sum(squares + counts * shift * shift, axis=0, keepdims=True)
         inverse = lax.rsqrt(square / total + epsilon)
         inv_ref[h] = inverse
@@ -243,7 +246,10 @@
         ]
         colpack_ref[h] = pad_rows(jnp.concatenate(rows, axis=0), LANES).T
 
-    def slabs(h):
+    size = width // 2
+    units = [(h, start) for h in range(hops) for start in (0, size)]
+
+    def slabs(h, start):
         rows = 16
 
         def slab(r):
@@ -256,27 +262,31 @@
             act[h, 0, rs, :] = high
             act[h, 1, rs, :] = low
 
-        return [functools.partial(slab, r) for r in range(0, width, rows)]
-
-    def products(h):
-        def product(start):
-            cols = slice(start, start + CHUNK)
-            high, low = act[h, 0, :, cols], act[h, 1, :, cols]
-            w2_high, w2_low = w2cat[h, :, :width], w2cat[h, :, width:]
-            value = dot(
-                jnp.concatenate([w2_high, w2_high, w2_low], axis=1),
-                jnp.concatenate([high, low, high], axis=0),
-            )
-            mid_ref[:, cols] = value if h == 0 else mid_ref[:, cols] + value
-
-        return [functools.partial(product, start) for start in range(0, nodes, CHUNK)]
-
-    for h in range(hops + 1):
-        if h < hops:
-            for copy in ready[h]:
+        return [functools.partial(slab, r) for r in range(start, start + size, rows)]
+
+    def products(h, start):
+        own = slice(start, start + size)
+        w2_high, w2_low = w2cat[h, :, own], w2cat[h, :, width + start : width + start + size]
+        w2_parts = jnp.concatenate([w2_high, w2_high, w2_low], axis=1)
+
+        def product(at):
+            cols = slice(at, at + CHUNK)
+            high, low = act[h, 0, own, cols], act[h, 1, own, cols]
+            value = dot(w2_parts, jnp.concatenate([high, low, high], axis=0))
+            mid_ref[:, cols] = value if (h, start) == units[0] else mid_ref[:, cols] + value
+
+        return [functools.partial(product, at) for at in range(0, nodes, CHUNK)]
+
+    for i in range(len(units) + 1):
+        if i < len(units) and units[i][1] == 0:
+            for copy in ready[units[i][0]]:
                 copy.wait()
-        weave(products(h - 1) if h else [lambda: None], slabs(h) if h < hops else [])
-        if h < hops:
+        weave(
+            products(*units[i - 1]) if i else [lambda: None],
+            slabs(*units[i]) if i < len(units) else [],
+        )
+        if i < len(units) and units[i][1] == size:
+            h = units[i][0]
             rows = slice(h * width, (h + 1) * width)
             copies.send(act.at[h, 0], act_hbm.at[0, rows, :])
             copies.send(act.at[h, 1], act_hbm.at[1, rows, :])
@@ -466,10 +476,10 @@
 
 
 def backward_kernel(
-    code_ref, pay_ref, inv_ref, gain_ref, bias_ref, colpack_ref, w_ref, gram_ref, misc_ref,
+    code_ref, pay_ref, inv_ref, gain_ref, colpack_ref, w_ref, gram_ref, misc_ref,
     g, w2_hbm, pre_hbm, xcat_hbm,
     pack_ref, feat_hbm,
-    w2, pre, xcat, feat, col, down, ucat, acc, prod, rows_scr, sems,
+    w2, pre, xcat, feat, col, down, ucat, acc, prod, rows_scr, shift_col, sems,
 ):
     copies = Copies(sems)
     hops, feats, width = w_ref.shape
@@ -532,8 +542,6 @@
         away1 = half1 * (1.0 - tan1)
         acc[two, 1, rs] += fold(grad1 * away1)
         grad = grad1 * (p1 + q1 * (tan1 + away1 * (1.0 + tan1)))
-        acc[two, 2, rs] += fold(grad)
-        acc[two, 3, rs] += fold(grad * half1)
         high, low = split(grad)
         ucat[two, rs, cs] = high
         ucat[two, width + r : width + r + rows, cs] = low
@@ -550,29 +558,29 @@
         low = dot_nt(xcat[h, :LANES, :], ucat[h % 2, width:, :])
         prod[h % 2] = value[:LANES] + value[LANES:] + low
 
+    def shifts(h):
+        shift = feature_shift(pay_ref, h)
+        rows_scr[h, :devices, :] = shift
+        rows_scr[h, devices:, :] = jnp.broadcast_to(real_nodes(pay_ref), shift.shape)
+        own_shift = rows_scr[h, pl.ds(code_ref[0], 1), :]
+        own_count = rows_scr[h, pl.ds(devices + code_ref[0], 1), :]
+        shift_col[h] = as_column(own_shift)
+        gram = gram_ref[h] + shift_col[h] * (own_shift * own_count)
+        pack_ref[h ^ flip, at + HEAD_ROWS :, :] = gram[:HOP_ROWS]
+
     def pack(h):
         two = h % 2
-        bias_sum = total_row(acc[two, 2])
-        shift = feature_shift(pay_ref, h)
-        rows_scr[:devices, :] = shift
-        rows_scr[devices:, :] = jnp.broadcast_to(real_nodes(pay_ref), shift.shape)
-        own_shift = rows_scr[pl.ds(code_ref[0], 1), :]
-        own_count = rows_scr[pl.ds(devices + code_ref[0], 1), :]
-        column = as_column(own_shift)
-        prod[two] = prod[two] + wide(column, mid) * bias_sum
-        prod[two, feats : feats + 1, :] = total_row(acc[two, 1])
-        prod[two, feats + 1 : feats + 2, :] = 2.0 * total_row(acc[two, 0])
-        prod[two, feats + 2 : feats + 3, :] = bias_sum
-        prod[two, feats + 3 : feats + 4, :] = (
-            2.0 * total_row(acc[two, 3]) - bias_ref[h] * bias_sum
-        ) / gain_ref[h]
+        bias_sum = prod[two, feats : feats + 1, :]
+        prod[two] = prod[two] + wide(shift_col[h], mid) * bias_sum
+        prod[two, feats + 1 : feats + 2, :] = total_row(acc[two, 1])
+        prod[two, feats + 2 : feats + 3, :] = 2.0 * total_row(acc[two, 0])
         for t in range(tiles):
             pack_ref[t ^ flip, h * HOP_ROWS : (h + 1) * HOP_ROWS, :] = prod[
                 two, :HOP_ROWS, t * LANES : (t + 1) * LANES
             ]
-        gram = gram_ref[h] + column * (own_shift * own_count)
-        pack_ref[h ^ flip, at + HEAD_ROWS :, :] = gram[:HOP_ROWS]
-
+
+    for h in range(hops):
+        shifts(h)
     rows = 16
     columns(0)
     w_in[0].wait()
@@ -594,10 +602,11 @@
             products += [functools.partial(feature_product, index - 1, part) for part in (0, 1)]
         if j == 0 and h >= 1:
             products.append(functools.partial(weight_product, h - 1))
+        slabs = [functools.partial(slab, index, r, rows) for r in range(0, width, rows)]
         if j == 1 and h >= 1:
             copies.send(feat.at[h - 1], feat_hbm.at[h - 1])
-            pack(h - 1)
-        weave(products, [functools.partial(slab, index, r, rows) for r in range(0, width, rows)])
+            slabs.insert(len(slabs) // 2, functools.partial(pack, h - 1))
+        weave(products, slabs)
     for part in (0, 1):
         feature_product(len(stages) - 1, part)
     copies.send(feat.at[hops - 1], feat_hbm.at[hops - 1])
@@ -642,15 +651,16 @@
         w = pad_rows(w_ref[h], LANES)
         inverse = inv_ref[h]
         scale = gain_ref[h] * inverse
-        slope1_out[h] = sum_ref[base + feats : base + feats + 1, :]
-        slope2_out[h] = sum_ref[base + feats + 1 : base + feats + 2, :]
-        bias_sum = sum_ref[base + feats + 2 : base + feats + 3, :]
-        gain_sum = sum_ref[base + feats + 3 : base + feats + 4, :]
+        bias_sum = sum_ref[base + feats : base + feats + 1, :]
+        slope1_out[h] = sum_ref[base + feats + 1 : base + feats + 2, :]
+        slope2_out[h] = sum_ref[base + feats + 2 : base + feats + 3, :]
+        products = sum_ref[base : base + feats, :]
+        gain_sum = inverse * jnp.sum(w_ref[h] * products, axis=0, keepdims=True)
         bias_out[h] = bias_sum
         gain_out[h] = gain_sum
         gram = sum_ref[at + HEAD_ROWS : at + HEAD_ROWS + HOP_ROWS, h * LANES : (h + 1) * LANES]
         inner = dot(gram, w, exact)[:feats] * (inverse * gain_sum / total)
-        wgrad[h] = scale * (sum_ref[base : base + feats, :] - inner)
+        wgrad[h] = scale * (products - inner)
         copies.send(wgrad.at[h], wgrad_hbm.at[:, h, :])
         shift = feature_shift(pay_ref, h)
         rows_scr[...] = shift
@@ -754,12 +764,12 @@
         in_specs=[anywhere, anywhere, vmem],
         out_specs=[vmem, vmem, anywhere, anywhere],
         out_shape=(
-            shape((devices, 24, LANES), f32), shape((hops, LANES, LANES), f32),
+            shape((devices, hops, width + LANES), f32), shape((hops, LANES, LANES), f32),
             shape((hops, 2 * LANES, nodes), bf16), shape((hops, feats, width), f32),
         ),
         scratch_shapes=[
             scratch(f32, hops, feats, nodes), scratch(f32, hops, feats, width),
-            scratch(bf16, hops, 2 * LANES, nodes), scratch(f32, 24, LANES), dma((4 * hops,)),
+            scratch(bf16, hops, 2 * LANES, nodes), scratch(f32, hops, width + LANES), dma((4 * hops,)),
         ],
         cost_estimate=cost(1_000_000_000, 8_000_000),
         name="first_stats",
@@ -849,21 +859,22 @@
     def backward(gcat):
         return call(
             backward_kernel,
-            52,
-            in_specs=[smem] + [vmem] * 9 + [anywhere] * 3,
+            46,
+            in_specs=[smem] + [vmem] * 8 + [anywhere] * 3,
             out_specs=[vmem, anywhere],
             scratch_shapes=[
                 scratch(f32, hops, width, mid), scratch(f32, hops, width, nodes),
                 scratch(bf16, hops, 2 * LANES, nodes),
                 scratch(f32, hops, feats, nodes), scratch(f32, 2, 6, width, LANES),
                 scratch(f32, 2, width, 2 * CHUNK), scratch(bf16, 2, 2 * width, nodes),
-                scratch(f32, 2, 4, width, LANES), scratch(f32, 2, LANES, mid),
-                scratch(f32, 2 * devices, LANES), dma((3 * hops + (hops + 1) * nodes // CHUNK,)),
+                scratch(f32, 2, 2, width, LANES), scratch(f32, 2, LANES, mid),
+                scratch(f32, hops, 2 * devices, LANES), scratch(f32, hops, LANES, LANES),
+                dma((3 * hops + (hops + 1) * nodes // CHUNK,)),
             ],
             out_shape=(shape((tiles, pack_rows, LANES), f32), shape((hops, feats, nodes), f32)),
             cost_estimate=cost(hops * 2 * 4 * width * mid * nodes, 24_000_000),
             name="backward",
-        )(place_code, pay, first_inv, gain, bias, colpack, w, gram, misc, gcat, mid_weight, pre, xcat)
+        )(place_code, pay, first_inv, gain, colpack, w, gram, misc, gcat, mid_weight, pre, xcat)
 
     a, b = kept[0] + came[0], kept[1] + came[1]
     size = a.shape[0] // 2

time: 214 us -> 203 us (0.949)
  Pallas kernels: 104 us -> 96.5 us
    pallas_call x1, Pallas kernels: 20.2 us -> 17 us  [on_device(): call(forward_kernel, 45, in_specs=[smem] + [vmem] * 7 + [anywhere] * 2, o...]
    pallas_call x1, Pallas kernels: 8.03 us -> 5.7 us  [on_device(): call(stats_kernel, 60, in_specs=[anywhere, anywhere, vmem], out_specs=[vm...]
    pallas_call x1, Pallas kernels: 31.4 us -> 29.2 us  [backward(): call(backward_kernel, 46, in_specs=[smem] + [vmem] * 8 + [anywhere] * 3,...]
  transfers between devices with their start and end apart: 23 -> 23, of which waited for: 12 -> 13; matrix products, arithmetic and copies ran while one was open for 0% -> 0% of each run, Pallas kernels for 29% -> 30%
where the time goes in v1:
time: 203 us; the launch traced here: 200 us
  Pallas kernels  96.5 us (48%)
  waiting for transfers between devices  46.2 us (23%)
  starting transfers between devices  30 us (15%)
  blocking collectives  21.8 us (11%)
  local copies, waits for them, and re-layouts  2.63 us (1%)
    ppermute x20, waiting for transfers between devices, exchange(): lax.ppermute(values, axes, [(i, i ^ 1 << bit) for i in range(devices)])  44.1 us
    pallas_call x1, Pallas kernels, backward(): call(backward_kernel, 46, in_specs=[smem] + [vmem] * 8 + [anywhere] * 3,...  29.2 us
    pallas_call x1, Pallas kernels, on_device(): call(forward_kernel, 45, in_specs=[smem] + [vmem] * 7 + [anywhere] * 2, o...  17 us
    ppermute x20, starting transfers between devices, exchange(): lax.ppermute(values, axes, [(i, i ^ 1 << bit) for i in range(devices)])  14.5 us
    all_to_all x1, blocking collectives, on_device(): stat = gather(stat)  11.8 us
    all_to_all x1, blocking collectives, on_device(): sums = gather(sums)  10 us
    pallas_call x1, Pallas kernels, on_device(): call(prepare_kernel, 60, in_specs=[anywhere, vmem, anywhere], out_specs=[...  9.63 us
    pallas_call x1, Pallas kernels, on_device(): call(finish_kernel, 60, in_specs=[smem] + [vmem] * 8 + [anywhere] * 2, ou...  9.11 us
  transfers between devices with their start and end apart: 23, of which 13 were waited for; matrix products, arithmetic and copies ran while one was open for 0% of the time, Pallas kernels for 30%

profile of v1, /device:TPU:0, one launch (start us, length us, event | category | flops | bytes accessed | tf_op | source)
XLA Modules:
  0.0 200.4 jit_solution(3842395752962857858)
XLA Ops:
  0.7 5.7 %first_stats.1 = (f32[32,4,640]{2,1,0:T(4,128)}, f32[4,128,128]{2,1,0:T(8,128)}, bf16[4,256,1536]{2,1,0:T(8,128)(2,1)}, f32[4,100,512]{2,1,0:T(8,128)}) custom-call(f32[100,4,1536]{2,1,0:T(4,128)} %bitcast.67, f32[100,4,512]{2,1,0:T(4,128)} %bitcast.69, s32[1536]{0:T(1024)} %mask_ref.9), custom_call_target="tpu_custom_call" | custom-call | flops 1000000000 | bytes 8000000 | tf_op jit(solution)/shard_map/first_stats/pallas_call | solution.py:761
  6.5 7.5 %all-to-all-start = ((f32[32,4,640]{2,1,0:T(4,128)}), f32[32,4,640]{2,1,0:T(4,128)S(1)}, u32[]{:S(2)}, u32[]{:S(2)}) async-start(f32[32,4,640]{2,1,0:T(4,128)} %get-tuple-element.78), calls=%async_computation | async-start | bytes 655360 | tf_op jit(solution)/shard_map/all_to_all | solution.py:777
  14.0 9.6 %prepare.1 = (f32[2048,1536]{1,0:T(8,128)}, bf16[4,512,1024]{2,1,0:T(8,128)(2,1)}) custom-call(bf16[4,256,1536]{2,1,0:T(8,128)(2,1)} %get-tuple-element.80.xcat_hbm, f32[4,100,512]{2,1,0:T(8,128)} %get-tuple-element.79.w_ref, f32[2048,512]{1,0:T(8,128)} %w2_hbm.3), custom_call_target="tpu_custom_call" | custom-call | flops 12884901888 | bytes 20000000 | tf_op jit(solution)/shard_map/prepare/pallas_call | solution.py:779
  23.6 2.1 %all-to-all-done.pay_ref = f32[32,4,640]{2,1,0:T(4,128)S(1)} async-done(((f32[32,4,640]{2,1,0:T(4,128)}), f32[32,4,640]{2,1,0:T(4,128)S(1)}, u32[]{:S(2)}, u32[]{:S(2)}) %all-to-all-start) | async-done | bytes 327712 | tf_op jit(solution)/shard_map/all_to_all | solution.py:777
  25.9 17.0 %forward.1 = (f32[512,1536]{1,0:T(8,128)S(1)}, f32[32,8,128]{2,1,0:T(8,128)S(1)}, f32[4,1,512]{2,1,0:T(1,128)S(1)}, f32[4,512,128]{2,1,0:T(8,128)S(1)}, bf16[2,2048,1536]{2,1,0:T(8,128)(2,1)}) custom-call(s32[2]{0:T(128)S(1)} %get-tuple-element.145.code_ref, f32[32,4,640]{2,1,0:T(4,128)S(1)} %all-to-all-done.pay_ref, f32[4,100,512]{2,1,0:T(8,128)S(1)} %copy-done.2, ...), custom_call_target="tpu_custom_call" | custom-call | flops 9663676416 | bytes 20000000 | tf_op jit(solution)/shard_map/forward/pallas_call | solution.py:793
  42.9 11.8 %all_to_all.25.stat_ref = f32[32,8,128]{2,1,0:T(8,128)S(1)} all-to-all(f32[32,8,128]{2,1,0:T(8,128)S(1)} %get-tuple-element.83), channel_id=1, replica_groups=mesh['dp'=8,'rep'=4] {'dp','rep'}, dimensions={0} | all-to-all | bytes 262144 | tf_op jit(solution)/shard_map/all_to_all | solution.py:810
  54.8 4.5 %head.1 = (f32[47,1536]{1,0:T(8,128)}, f32[1,512]{1,0:T(1,128)S(1)}, f32[32,8,128]{2,1,0:T(8,128)S(1)}, f32[4,56,128]{2,1,0:T(8,128)S(1)}, f32[512,1536]{1,0:T(8,128)S(1)}, /*index=5*/f32[512,1536]{1,0:T(8,128)S(1)}) custom-call(f32[32,4,640]{2,1,0:T(4,128)S(1)} %all-to-all-done.pay_ref, f32[32,8,128]{2,1,0:T(8,128)S(1)} %all_to_all.25.stat_ref, ...), custom_call_target="tpu_custom_call" | custom-call | flops 2000000000 | bytes 10000000 | tf_op jit(solution)/shard_map/head/pallas_call | solution.py:812
  59.3 10.0 %all_to_all.26.sums_ref = f32[32,8,128]{2,1,0:T(8,128)S(1)} all-to-all(f32[32,8,128]{2,1,0:T(8,128)S(1)} %get-tuple-element.87), channel_id=1, replica_groups=mesh['dp'=8,'rep'=4] {'dp','rep'}, dimensions={0} | all-to-all | bytes 262144 | tf_op jit(solution)/shard_map/all_to_all | solution.py:830
  69.3 7.9 %mid_grad_send.1 = (f32[2,512,512]{2,1,0:T(8,128)S(1)}, f32[2,512]{1,0:T(2,128)S(1)}, bf16[1024,1536]{1,0:T(8,128)(2,1)S(1)}) custom-call(s32[2]{0:T(128)S(1)} %get-tuple-element.144.code_ref, f32[32,4,640]{2,1,0:T(4,128)S(1)} %all-to-all-done.pay_ref, f32[32,8,128]{2,1,0:T(8,128)S(1)} %all_to_all.26.sums_ref, f32[1,512]{1,0:T(1,128)S(1)} %get-tuple-element.88.inv_ref, ...), custom_call_target="tpu_custom_call" | custom-call | flops 4831838208 | bytes 10000000 | tf_op jit(solution)/shard_map/mid_grad_send/pallas_call | solution.py:833
  78.0 8.0 %mid_grad_keep.1 = f32[2,512,512]{2,1,0:T(8,128)S(1)} custom-call(s32[2]{0:T(128)S(1)} %get-tuple-element.144.code_ref, bf16[1024,1536]{1,0:T(8,128)(2,1)S(1)} %get-tuple-element.97.gcat.g, bf16[2,2048,1536]{2,1,0:T(8,128)(2,1)} %get-tuple-element.91.act_hbm), custom_call_target="tpu_custom_call" | custom-call | flops 4831838208 | bytes 10000000 | tf_op jit(solution)/shard_map/mid_grad_keep/pallas_call | solution.py:846
  88.2 29.2 %backward.1 = (f32[4,576,128]{2,1,0:T(8,128)S(1)}, f32[4,100,1536]{2,1,0:T(8,128)S(1)}) custom-call(s32[2]{0:T(128)S(1)} %get-tuple-element.145.code_ref, f32[32,4,640]{2,1,0:T(4,128)S(1)} %all-to-all-done.pay_ref, f32[4,1,512]{2,1,0:T(1,128)S(1)} %get-tuple-element.86.inv_ref, f32[4,1,512]{2,1,0:T(1,128)S(1)} %bitcast.47, ...), custom_call_target="tpu_custom_call" | custom-call | flops 12884901888 | bytes 24000000 | tf_op jit(solution)/shard_map/backward/pallas_call | solution.py:860
  117.7 2.0 collective-permute-done.3
  123.3 3.5 %all-to-all-start.3 = ((f32[8,144,128]{2,1,0:T(8,128)}), f32[8,144,128]{2,1,0:T(8,128)S(1)}, u32[]{:S(2)}, u32[]{:S(2)}) async-start(f32[8,144,128]{2,1,0:T(8,128)} %bitcast.19), calls=%async_computation.3 | async-start | bytes 1179648 | tf_op jit(solution)/shard_map/all_to_all | solution.py:899
  126.8 2.2 %collective-permute-done.4 = f32[128,512]{1,0:T(8,128)S(1)} collective-permute-done((f32[128,512]{1,0:T(8,128)S(1)}, f32[128,512]{1,0:T(8,128)S(1)}, u32[]{:S(2)}, u32[]{:S(2)}) %collective-permute-start.4) | collective-permute-done | bytes 262176 | tf_op jit(solution)/shard_map/ppermute | solution.py:698
  129.0 3.3 %collective-permute-done.5 = f32[128,512]{1,0:T(8,128)S(1)} collective-permute-done((f32[128,512]{1,0:T(8,128)S(1)}, f32[128,512]{1,0:T(8,128)S(1)}, u32[]{:S(2)}, u32[]{:S(2)}) %collective-permute-start.5) | collective-permute-done | bytes 262176 | tf_op jit(solution)/shard_map/ppermute | solution.py:698
  133.1 8.0 %collective-permute-done.6 = f32[2,2,32,512]{3,2,0,1:T(8,128)S(1)} collective-permute-done((f32[2,2,32,512]{3,2,0,1:T(8,128)S(1)}, f32[2,2,32,512]{3,2,0,1:T(8,128)S(1)}, u32[]{:S(2)}, u32[]{:S(2)}) %collective-permute-start.6) | collective-permute-done | bytes 262176 | tf_op jit(solution)/shard_map/ppermute | solution.py:698
  142.1 2.1 %collective-permute-start.8 = (f32[144,128]{1,0:T(8,128)S(1)}, f32[144,128]{1,0:T(8,128)S(1)}, u32[]{:S(2)}, u32[]{:S(2)}) collective-permute-start(f32[144,128]{1,0:T(8,128)S(1)} %reduce_sum.9), channel_id=1, source_target_pairs={{0,16},{1,17},{2,18},{3,19},{4,20},{5,21},{6,22},{7,23},{8,24},{9,... | collective-permute-start | bytes 221192 | tf_op jit(solution)/shard_map/ppermute | solution.py:698
  144.2 8.0 %collective-permute-done.8 = f32[144,128]{1,0:T(8,128)S(1)} collective-permute-done((f32[144,128]{1,0:T(8,128)S(1)}, f32[144,128]{1,0:T(8,128)S(1)}, u32[]{:S(2)}, u32[]{:S(2)}) %collective-permute-start.8) | collective-permute-done | bytes 73760 | tf_op jit(solution)/shard_map/ppermute | solution.py:698
  153.1 4.4 %all-to-all-start.4 = ((f32[8,144,128]{2,1,0:T(8,128)}), f32[8,144,128]{2,1,0:T(8,128)S(1)}, u32[]{:S(2)}, u32[]{:S(2)}) async-start(f32[8,144,128]{2,1,0:T(8,128)} %broadcast_in_dim.2), calls=%async_computation.4 | async-start | bytes 1179648 | tf_op jit(solution)/shard_map/all_to_all | solution.py:913
  157.5 1.9 collective-permute-done.10
  159.7 11.7 %collective-permute-done.11 = f32[2,2,32,512]{3,2,0,1:T(8,128)S(1)} collective-permute-done((f32[2,2,32,512]{3,2,0,1:T(8,128)S(1)}, f32[2,2,32,512]{3,2,0,1:T(8,128)S(1)}, u32[]{:S(2)}, u32[]{:S(2)}) %collective-permute-start.11) | collective-permute-done | bytes 262176 | tf_op jit(solution)/shard_map/ppermute | solution.py:698
  174.7 3.4 %collective-permute-done.12 = f32[128,512]{1,0:T(8,128)S(1)} collective-permute-done((f32[128,512]{1,0:T(8,128)S(1)}, f32[128,512]{1,0:T(8,128)S(1)}, u32[]{:S(2)}, u32[]{:S(2)}) %collective-permute-start.12) | collective-permute-done | bytes 262176 | tf_op jit(solution)/shard_map/ppermute | solution.py:698
  183.0 9.1 %finish.1 = (f32[100,4,1536]{2,1,0:T(4,128)}, f32[100,4,512]{2,1,0:T(4,128)}, f32[4,1,512]{2,1,0:T(1,128)}, f32[4,1,512]{2,1,0:T(1,128)}, f32[4,1,512]{2,1,0:T(1...) custom-call(s32[2]{0:T(128)} %copy-done.8, ...), custom_call_target="tpu_custom_call" | custom-call | bytes 20000000 | tf_op jit(solution)/shard_map/finish/pallas_call | solution.py:930
  192.2 2.1 %place.3.refs_2_ = f32[2048,512]{1,0:T(8,128)} custom-call(s32[2]{0:T(128)S(1)} %get-tuple-element.144.code_ref, f32[256,512]{1,0:T(8,128)S(1)} %pad_maximum_fusion.refs_0_, f32[256,512]{1,0:T(8,128)S(1)} %pad_maximum_fusion.1.refs_1_, f32[256,512]{1,0:T(8,128)S(1)} %collective-permute-done.16.refs_2_, f32[256,512]{1,0:T(8,128)S(1)} %collective-permute-done.17.refs_3_), custom_call_target="tpu_custom_call" | custom-call | bytes 4000000 | tf_op jit(solution)/shard_map/place/pallas_call | solution.py:954
  (103 shorter events, 23.8 us)
Async XLA Ops:
  6.4 81.7 %copy-start.8 = (s32[2]{0:T(128)}, s32[2]{0:T(128)S(1)}, u32[]{:S(2)}) copy-start(s32[2]{0:T(128)S(1)} %get-tuple-element.145.code_ref) | copy-start | bytes 28
  6.5 19.3 %all-to-all-start = ((f32[32,4,640]{2,1,0:T(4,128)}), f32[32,4,640]{2,1,0:T(4,128)S(1)}, u32[]{:S(2)}, u32[]{:S(2)}) async-start(f32[32,4,640]{2,1,0:T(4,128)} %get-tuple-element.78), calls=%async_computation | async-start | bytes 655360 | tf_op jit(solution)/shard_map/all_to_all | solution.py:777
  77.8 8.2 %collective-permute-start = (f32[2,512,512]{2,1,0:T(8,128)S(1)}, f32[2,512,512]{2,1,0:T(8,128)S(1)}, u32[]{:S(2)}, u32[]{:S(2)}) collective-permute-start(f32[2,512,512]{2,1,0:T(8,128)S(1)} %get-tuple-element.93), channel_id=1, source_target_pairs={{0,1},{1,0},{2,3},{3,2},{4,5},{5,4},{6,7},{7,6},{8,9},{9,8},{10,11... | collective-permute-start | bytes 6291464 | tf_op jit(solution)/shard_map/ppermute | solution.py:698
  86.6 30.7 %collective-permute-start.1 = (f32[256,512]{1,0:T(8,128)S(1)}, f32[256,512]{1,0:T(8,128)S(1)}, u32[]{:S(2)}, u32[]{:S(2)}) collective-permute-start(f32[256,512]{1,0:T(8,128)S(1)} %slice_bitcast_fusion.2), channel_id=1, source_target_pairs={{0,2},{1,3},{2,0},{3,1},{4,6},{5,7},{6,4},{7,5},{8,10},{9,11},{10,... | collective-permute-start | bytes 1572872 | tf_op jit(solution)/shard_map/ppermute | solution.py:698
  87.1 30.3 %collective-permute-start.2 = (f32[256,512]{1,0:T(8,128)S(1)}, f32[256,512]{1,0:T(8,128)S(1)}, u32[]{:S(2)}, u32[]{:S(2)}) collective-permute-start(f32[256,512]{1,0:T(8,128)S(1)} %slice_bitcast_fusion.1), channel_id=1, source_target_pairs={{0,4},{1,5},{2,6},{3,7},{4,0},{5,1},{6,2},{7,3},{8,12},{9,13},{10,... | collective-permute-start | bytes 1572872 | tf_op jit(solution)/shard_map/ppermute | solution.py:698
  117.6 2.1 %collective-permute-start.3 = (f32[2,576,128]{2,1,0:T(8,128)S(1)}, f32[2,576,128]{2,1,0:T(8,128)S(1)}, u32[]{:S(2)}, u32[]{:S(2)}) collective-permute-start(f32[2,576,128]{2,1,0:T(8,128)S(1)} %slice.85), channel_id=1, source_target_pairs={{0,1},{1,0},{2,3},{3,2},{4,5},{5,4},{6,7},{7,6},{8,9},{9,8},{10,11... | collective-permute-start | bytes 1769480 | tf_op jit(solution)/shard_map/ppermute | solution.py:698
  120.6 8.4 %collective-permute-start.4 = (f32[128,512]{1,0:T(8,128)S(1)}, f32[128,512]{1,0:T(8,128)S(1)}, u32[]{:S(2)}, u32[]{:S(2)}) collective-permute-start(f32[128,512]{1,0:T(8,128)S(1)} %slice.87), channel_id=1, source_target_pairs={{0,4},{1,5},{2,6},{3,7},{4,0},{5,1},{6,2},{7,3},{8,12},{9,13},{10,... | collective-permute-start | bytes 786440 | tf_op jit(solution)/shard_map/ppermute | solution.py:698
  121.7 10.7 %collective-permute-start.5 = (f32[128,512]{1,0:T(8,128)S(1)}, f32[128,512]{1,0:T(8,128)S(1)}, u32[]{:S(2)}, u32[]{:S(2)}) collective-permute-start(f32[128,512]{1,0:T(8,128)S(1)} %slice.88), channel_id=1, source_target_pairs={{0,2},{1,3},{2,0},{3,1},{4,6},{5,7},{6,4},{7,5},{8,10},{9,11},{10,... | collective-permute-start | bytes 786440 | tf_op jit(solution)/shard_map/ppermute | solution.py:698
  123.3 17.9 %all-to-all-start.3 = ((f32[8,144,128]{2,1,0:T(8,128)}), f32[8,144,128]{2,1,0:T(8,128)S(1)}, u32[]{:S(2)}, u32[]{:S(2)}) async-start(f32[8,144,128]{2,1,0:T(8,128)} %bitcast.19), calls=%async_computation.3 | async-start | bytes 1179648 | tf_op jit(solution)/shard_map/all_to_all | solution.py:899
  132.4 8.6 %collective-permute-start.6 = (f32[2,2,32,512]{3,2,0,1:T(8,128)S(1)}, f32[2,2,32,512]{3,2,0,1:T(8,128)S(1)}, u32[]{:S(2)}, u32[]{:S(2)}) collective-permute-start(f32[2,2,32,512]{3,2,0,1:T(8,128)S(1)} %pad_maximum_fusion.2), channel_id=1, source_target_pairs={{0,8},{1,9},{2,10},{3,11},{4,12},{5,13},{6,14},{7,15},{8,0},{9,1},... | collective-permute-start | bytes 786440 | tf_op jit(solution)/shard_map/ppermute | solution.py:698
  141.2 11.0 %collective-permute-start.7 = (f32[1,2,32,512]{3,2,0,1:T(8,128)S(1)}, f32[1,2,32,512]{3,2,0,1:T(8,128)S(1)}, u32[]{:S(2)}, u32[]{:S(2)}) collective-permute-start(f32[1,2,32,512]{3,2,0,1:T(8,128)S(1)} %slice.92), channel_id=1, source_target_pairs={{0,16},{1,17},{2,18},{3,19},{4,20},{5,21},{6,22},{7,23},{8,24},{9,... | collective-permute-start | bytes 393224 | tf_op jit(solution)/shard_map/ppermute | solution.py:698
  142.1 10.1 %collective-permute-start.8 = (f32[144,128]{1,0:T(8,128)S(1)}, f32[144,128]{1,0:T(8,128)S(1)}, u32[]{:S(2)}, u32[]{:S(2)}) collective-permute-start(f32[144,128]{1,0:T(8,128)S(1)} %reduce_sum.9), channel_id=1, source_target_pairs={{0,16},{1,17},{2,18},{3,19},{4,20},{5,21},{6,22},{7,23},{8,24},{9,... | collective-permute-start | bytes 221192 | tf_op jit(solution)/shard_map/ppermute | solution.py:698
  153.1 6.3 %collective-permute-start.10 = (f32[1,2,32,512]{3,2,0,1:T(8,128)S(1)}, f32[1,2,32,512]{3,2,0,1:T(8,128)S(1)}, u32[]{:S(2)}, u32[]{:S(2)}) collective-permute-start(f32[1,2,32,512]{3,2,0,1:T(8,128)S(1)} %slice_add_fusion.5), channel_id=1, source_target_pairs={{0,16},{1,17},{2,18},{3,19},{4,20},{5,21},{6,22},{7,23},{8,24},{9,... | collective-permute-start | bytes 393224 | tf_op jit(solution)/shard_map/ppermute | solution.py:698
  153.1 26.5 %all-to-all-start.4 = ((f32[8,144,128]{2,1,0:T(8,128)}), f32[8,144,128]{2,1,0:T(8,128)S(1)}, u32[]{:S(2)}, u32[]{:S(2)}) async-start(f32[8,144,128]{2,1,0:T(8,128)} %broadcast_in_dim.2), calls=%async_computation.4 | async-start | bytes 1179648 | tf_op jit(solution)/shard_map/all_to_all | solution.py:913
  159.4 12.0 %collective-permute-start.11 = (f32[2,2,32,512]{3,2,0,1:T(8,128)S(1)}, f32[2,2,32,512]{3,2,0,1:T(8,128)S(1)}, u32[]{:S(2)}, u32[]{:S(2)}) collective-permute-start(f32[2,2,32,512]{3,2,0,1:T(8,128)S(1)} %pad_maximum_fusion.3), channel_id=1, source_target_pairs={{0,8},{1,9},{2,10},{3,11},{4,12},{5,13},{6,14},{7,15},{8,0},{9,1},... | collective-permute-start | bytes 786440 | tf_op jit(solution)/shard_map/ppermute | solution.py:698
  171.4 6.6 %collective-permute-start.12 = (f32[128,512]{1,0:T(8,128)S(1)}, f32[128,512]{1,0:T(8,128)S(1)}, u32[]{:S(2)}, u32[]{:S(2)}) collective-permute-start(f32[128,512]{1,0:T(8,128)S(1)} %bitcast.65), channel_id=1, source_target_pairs={{0,4},{1,5},{2,6},{3,7},{4,0},{5,1},{6,2},{7,3},{8,12},{9,13},{10,... | collective-permute-start | bytes 786440 | tf_op jit(solution)/shard_map/ppermute | solution.py:698
  173.2 6.4 %collective-permute-start.13 = (f32[128,512]{1,0:T(8,128)S(1)}, f32[128,512]{1,0:T(8,128)S(1)}, u32[]{:S(2)}, u32[]{:S(2)}) collective-permute-start(f32[128,512]{1,0:T(8,128)S(1)} %bitcast.63), channel_id=1, source_target_pairs={{0,2},{1,3},{2,0},{3,1},{4,6},{5,7},{6,4},{7,5},{8,10},{9,11},{10,... | collective-permute-start | bytes 786440 | tf_op jit(solution)/shard_map/ppermute | solution.py:698
  179.6 2.5 %collective-permute-start.9 = (f32[2,576,128]{2,1,0:T(8,128)S(1)}, f32[2,576,128]{2,1,0:T(8,128)S(1)}, u32[]{:S(2)}, u32[]{:S(2)}) collective-permute-start(f32[2,576,128]{2,1,0:T(8,128)S(1)} %bitcast.57), channel_id=1, source_target_pairs={{0,1},{1,0},{2,3},{3,2},{4,5},{5,4},{6,7},{7,6},{8,9},{9,8},{10,11... | collective-permute-start | bytes 1769480 | tf_op jit(solution)/shard_map/ppermute | solution.py:698
  179.8 12.4 %collective-permute-start.17 = (f32[256,512]{1,0:T(8,128)S(1)}, f32[256,512]{1,0:T(8,128)S(1)}, u32[]{:S(2)}, u32[]{:S(2)}) collective-permute-start(f32[256,512]{1,0:T(8,128)S(1)} %pad_maximum_fusion.1.refs_1_), channel_id=1, source_target_pairs={{0,1},{1,0},{2,3},{3,2},{4,5},{5,4},{6,7},{7,6},{8,9},{9,8},{10,11... | collective-permute-start | bytes 1572872 | tf_op jit(solution)/shard_map/ppermute | solution.py:698
  180.3 11.8 %collective-permute-start.16 = (f32[256,512]{1,0:T(8,128)S(1)}, f32[256,512]{1,0:T(8,128)S(1)}, u32[]{:S(2)}, u32[]{:S(2)}) collective-permute-start(f32[256,512]{1,0:T(8,128)S(1)} %pad_maximum_fusion.refs_0_), channel_id=1, source_target_pairs={{0,1},{1,0},{2,3},{3,2},{4,5},{5,4},{6,7},{7,6},{8,9},{9,8},{10,11... | collective-permute-start | bytes 1572872 | tf_op jit(solution)/shard_map/ppermute | solution.py:698
  180.4 14.3 %collective-permute-start.14 = (f32[256,512]{1,0:T(8,128)S(1)}, f32[256,512]{1,0:T(8,128)S(1)}, u32[]{:S(2)}, u32[]{:S(2)}) collective-permute-start(f32[256,512]{1,0:T(8,128)S(1)} %pad_maximum_fusion.refs_0_), channel_id=1, source_target_pairs={{0,2},{1,3},{2,0},{3,1},{4,6},{5,7},{6,4},{7,5},{8,10},{9,11},{10,... | collective-permute-start | bytes 1572872 | tf_op jit(solution)/shard_map/ppermute | solution.py:698
  181.9 14.0 %collective-permute-start.15 = (f32[256,512]{1,0:T(8,128)S(1)}, f32[256,512]{1,0:T(8,128)S(1)}, u32[]{:S(2)}, u32[]{:S(2)}) collective-permute-start(f32[256,512]{1,0:T(8,128)S(1)} %pad_maximum_fusion.1.refs_1_), channel_id=1, source_target_pairs={{0,4},{1,5},{2,6},{3,7},{4,0},{5,1},{6,2},{7,3},{8,12},{9,13},{10,... | collective-permute-start | bytes 1572872 | tf_op jit(solution)/shard_map/ppermute | solution.py:698
  195.9 2.2 %collective-permute-start.19 = (f32[256,512]{1,0:T(8,128)S(1)}, f32[256,512]{1,0:T(8,128)S(1)}, u32[]{:S(2)}, u32[]{:S(2)}) collective-permute-start(f32[256,512]{1,0:T(8,128)S(1)} %collective-permute-done.15.refs_1_), channel_id=1, source_target_pairs={{0,1},{1,0},{2,3},{3,2},{4,5},{5,4},{6,7},{7,6},{8,9},{9,8},{10,11... | collective-permute-start | bytes 1572872 | tf_op jit(solution)/shard_map/ppermute | solution.py:698
  195.9 2.7 %collective-permute-start.18 = (f32[256,512]{1,0:T(8,128)S(1)}, f32[256,512]{1,0:T(8,128)S(1)}, u32[]{:S(2)}, u32[]{:S(2)}) collective-permute-start(f32[256,512]{1,0:T(8,128)S(1)} %collective-permute-done.14.refs_0_), channel_id=1, source_target_pairs={{0,1},{1,0},{2,3},{3,2},{4,5},{5,4},{6,7},{7,6},{8,9},{9,8},{10,11... | collective-permute-start | bytes 1572872 | tf_op jit(solution)/shard_map/ppermute | solution.py:698
  (20 other events, 370.3 us)

commit v2 on v1

--- a/solution.py
+++ b/solution.py
@@ -462,9 +462,11 @@
             for copy in ready[s * 2 + r]:
                 copy.wait()
             here = slice(r * size, (r + 1) * size)
-            value = dot_nt(act[s, 0, here, :], gcat[:mid, :])
-            value = value + dot_nt(act[s, 0, here, :], gcat[mid:, :])
-            value = value + dot_nt(act[s, 1, here, :], gcat[:mid, :])
+            high, low = act[s, 0, here, :], act[s, 1, here, :]
+            value = dot_nt(
+                jnp.concatenate([high, high, low], axis=1),
+                jnp.concatenate([gcat[:mid, :], gcat[mid:, :], gcat[:mid, :]], axis=1),
+            )
             for i in range(size // rows):
                 place = (r * (size // rows) + i) ^ code
                 out_ref[s, aligned(place, rows), :] = value[i * rows : (i + 1) * rows]
@@ -477,9 +479,9 @@
 
 def backward_kernel(
     code_ref, pay_ref, inv_ref, gain_ref, colpack_ref, w_ref, gram_ref, misc_ref,
-    g, w2_hbm, pre_hbm, xcat_hbm,
+    g, w2, pre_hbm, xcat_hbm,
     pack_ref, feat_hbm,
-    w2, pre, xcat, feat, col, down, ucat, acc, prod, rows_scr, shift_col, sems,
+    pre, xcat, feat, col, down, ucat, acc, prod, rows_scr, shift_col, sems,
 ):
     copies = Copies(sems)
     hops, feats, width = w_ref.shape
@@ -489,10 +491,9 @@
     chunks = [slice(start, start + size) for start in range(0, nodes, size)]
     count = len(chunks)
     stages = [(h, j) for h in range(hops) for j in range(count)]
-    w_in, z_in, x_in = {}, {}, {}
+    z_in, x_in = {}, {}
     for h in range(hops):
         own = slice(h * width, (h + 1) * width)
-        w_in[h] = copies.start(w2_hbm.at[own, :], w2.at[h])
         for j, c in enumerate(chunks):
             z_in[h, j] = copies.start(pre_hbm.at[own, c], pre.at[h, :, c])
         x_in[h] = copies.start(xcat_hbm.at[h], xcat.at[h])
@@ -508,12 +509,11 @@
         for r in range(0, width, rows):
             for k, values in enumerate(columns_of(colpack_ref[h, r : r + rows, :])):
                 col[h % 2, k, r : r + rows, :] = values
-        acc[h % 2] = jnp.zeros(acc.shape[1:], f32)
 
     def weights(h):
         high, low = split(pad_rows(w_ref[h], LANES) * (gain_ref[h] * inv_ref[h]))
         wcat[h] = (jnp.concatenate([high, low], axis=0), high)
-        high, low = split(0.5 * w2[h])
+        high, low = split(0.5 * w2[h * width : (h + 1) * width, :])
         w2cat[h] = jnp.concatenate([high, high, low], axis=1)
 
     def part_of(j, part):
@@ -537,14 +537,17 @@
         half2 = half1 * (p1 + q1 * tan1)
         tan2 = jnp.tanh(half2)
         away2 = half2 * (1.0 - tan2)
-        acc[two, 0, rs] += fold(grad2 * away2)
+        add(acc, two, 0, rs, j, fold(grad2 * away2))
         grad1 = grad2 * (p2 + q2 * (tan2 + away2 * (1.0 + tan2)))
         away1 = half1 * (1.0 - tan1)
-        acc[two, 1, rs] += fold(grad1 * away1)
+        add(acc, two, 1, rs, j, fold(grad1 * away1))
         grad = grad1 * (p1 + q1 * (tan1 + away1 * (1.0 + tan1)))
         high, low = split(grad)
         ucat[two, rs, cs] = high
         ucat[two, width + r : width + r + rows, cs] = low
+
+    def add(acc, two, k, rs, j, value):
+        acc[two, k, rs] = value if j == 0 else acc[two, k, rs] + value
 
     def feature_product(index, part):
         h, j = stages[index]
@@ -579,31 +582,29 @@
                 two, :HOP_ROWS, t * LANES : (t + 1) * LANES
             ]
 
-    for h in range(hops):
-        shifts(h)
     rows = 16
-    columns(0)
-    w_in[0].wait()
     weights(0)
-    for part in (0, 1):
-        down_product(0, part)
+    weave(
+        [functools.partial(down_product, 0, part) for part in (0, 1)],
+        [functools.partial(columns, 0)] + [functools.partial(shifts, h) for h in range(hops)],
+    )
     for index, (h, j) in enumerate(stages):
         products = []
         z_in[h, j].wait()
         if j + 1 == count:
             x_in[h].wait()
             if h + 1 < hops:
-                w_in[h + 1].wait()
                 weights(h + 1)
                 columns(h + 1)
         if index + 1 < len(stages):
             products += [functools.partial(down_product, index + 1, part) for part in (0, 1)]
         if index >= 1:
-            products += [functools.partial(feature_product, index - 1, part) for part in (0, 1)]
-        if j == 0 and h >= 1:
+            before = [functools.partial(feature_product, index - 1, part) for part in (0, 1)]
+            products = before + products
+        if j == 1 and h >= 1:
             products.append(functools.partial(weight_product, h - 1))
         slabs = [functools.partial(slab, index, r, rows) for r in range(0, width, rows)]
-        if j == 1 and h >= 1:
+        if j == 2 and h >= 1:
             copies.send(feat.at[h - 1], feat_hbm.at[h - 1])
             slabs.insert(len(slabs) // 2, functools.partial(pack, h - 1))
         weave(products, slabs)
@@ -859,12 +860,11 @@
     def backward(gcat):
         return call(
             backward_kernel,
-            46,
-            in_specs=[smem] + [vmem] * 8 + [anywhere] * 3,
+            42,
+            in_specs=[smem] + [vmem] * 9 + [anywhere] * 2,
             out_specs=[vmem, anywhere],
             scratch_shapes=[
-                scratch(f32, hops, width, mid), scratch(f32, hops, width, nodes),
-                scratch(bf16, hops, 2 * LANES, nodes),
+                scratch(f32, hops, width, nodes), scratch(bf16, hops, 2 * LANES, nodes),
                 scratch(f32, hops, feats, nodes), scratch(f32, 2, 6, width, LANES),
                 scratch(f32, 2, width, 2 * CHUNK), scratch(bf16, 2, 2 * width, nodes),
                 scratch(f32, 2, 2, width, LANES), scratch(f32, 2, LANES, mid),

time: 203 us -> 200 us (0.985)
  Pallas kernels: 96.5 us -> 93.3 us
    pallas_call x1, Pallas kernels: 29.2 us -> 26.6 us  [backward(): call(backward_kernel, 42, in_specs=[smem] + [vmem] * 9 + [anywhere] * 2,...]
  transfers between devices with their start and end apart: 23 -> 23, of which waited for: 13 -> 13; matrix products, arithmetic and copies ran while one was open for 0% -> 0% of each run, Pallas kernels for 30% -> 29%
where the time goes in v2:
time: 200 us; the launch traced here: 197 us
  Pallas kernels  93.3 us (47%)
  waiting for transfers between devices  46.9 us (23%)
  starting transfers between devices  29 us (14%)
  blocking collectives  21.8 us (11%)
  local copies, waits for them, and re-layouts  2.61 us (1%)
    ppermute x20, waiting for transfers between devices, exchange(): lax.ppermute(values, axes, [(i, i ^ 1 << bit) for i in range(devices)])  44.8 us
    pallas_call x1, Pallas kernels, backward(): call(backward_kernel, 42, in_specs=[smem] + [vmem] * 9 + [anywhere] * 2,...  26.6 us
    pallas_call x1, Pallas kernels, on_device(): call(forward_kernel, 45, in_specs=[smem] + [vmem] * 7 + [anywhere] * 2, o...  17 us
    ppermute x20, starting transfers between devices, exchange(): lax.ppermute(values, axes, [(i, i ^ 1 << bit) for i in range(devices)])  13.8 us
    all_to_all x1, blocking collectives, on_device(): stat = gather(stat)  11.8 us
    all_to_all x1, blocking collectives, on_device(): sums = gather(sums)  10 us
    pallas_call x1, Pallas kernels, on_device(): call(prepare_kernel, 60, in_specs=[anywhere, vmem, anywhere], out_specs=[...  9.63 us
    pallas_call x1, Pallas kernels, on_device(): call(finish_kernel, 60, in_specs=[smem] + [vmem] * 8 + [anywhere] * 2, ou...  9.11 us
  transfers between devices with their start and end apart: 23, of which 13 were waited for; matrix products, arithmetic and copies ran while one was open for 0% of the time, Pallas kernels for 29%

profile of v2, /device:TPU:0, one launch (start us, length us, event | category | flops | bytes accessed | tf_op | source)
XLA Modules:
  0.0 197.1 jit_solution(11384033391861080658)
XLA Ops:
  0.7 5.7 %first_stats.1 = (f32[32,4,640]{2,1,0:T(4,128)}, f32[4,128,128]{2,1,0:T(8,128)}, bf16[4,256,1536]{2,1,0:T(8,128)(2,1)}, f32[4,100,512]{2,1,0:T(8,128)}) custom-call(f32[100,4,1536]{2,1,0:T(4,128)} %bitcast.67, f32[100,4,512]{2,1,0:T(4,128)} %bitcast.69, s32[1536]{0:T(1024)} %mask_ref.9), custom_call_target="tpu_custom_call" | custom-call | flops 1000000000 | bytes 8000000 | tf_op jit(solution)/shard_map/first_stats/pallas_call | solution.py:762
  6.5 7.5 %all-to-all-start = ((f32[32,4,640]{2,1,0:T(4,128)}), f32[32,4,640]{2,1,0:T(4,128)S(1)}, u32[]{:S(2)}, u32[]{:S(2)}) async-start(f32[32,4,640]{2,1,0:T(4,128)} %get-tuple-element.78), calls=%async_computation | async-start | bytes 655360 | tf_op jit(solution)/shard_map/all_to_all | solution.py:778
  14.0 9.6 %prepare.1 = (f32[2048,1536]{1,0:T(8,128)}, bf16[4,512,1024]{2,1,0:T(8,128)(2,1)}) custom-call(bf16[4,256,1536]{2,1,0:T(8,128)(2,1)} %get-tuple-element.80.xcat_hbm, f32[4,100,512]{2,1,0:T(8,128)} %get-tuple-element.79.w_ref, f32[2048,512]{1,0:T(8,128)} %w2.1), custom_call_target="tpu_custom_call" | custom-call | flops 12884901888 | bytes 20000000 | tf_op jit(solution)/shard_map/prepare/pallas_call | solution.py:780
  23.6 2.1 %all-to-all-done.pay_ref = f32[32,4,640]{2,1,0:T(4,128)S(1)} async-done(((f32[32,4,640]{2,1,0:T(4,128)}), f32[32,4,640]{2,1,0:T(4,128)S(1)}, u32[]{:S(2)}, u32[]{:S(2)}) %all-to-all-start) | async-done | bytes 327712 | tf_op jit(solution)/shard_map/all_to_all | solution.py:778
  25.9 17.0 %forward.1 = (f32[512,1536]{1,0:T(8,128)S(1)}, f32[32,8,128]{2,1,0:T(8,128)S(1)}, f32[4,1,512]{2,1,0:T(1,128)S(1)}, f32[4,512,128]{2,1,0:T(8,128)S(1)}, bf16[2,2048,1536]{2,1,0:T(8,128)(2,1)}) custom-call(s32[2]{0:T(128)S(1)} %get-tuple-element.145.code_ref, f32[32,4,640]{2,1,0:T(4,128)S(1)} %all-to-all-done.pay_ref, f32[4,100,512]{2,1,0:T(8,128)S(1)} %copy-done.2, ...), custom_call_target="tpu_custom_call" | custom-call | flops 9663676416 | bytes 20000000 | tf_op jit(solution)/shard_map/forward/pallas_call | solution.py:794
  42.9 11.8 %all_to_all.25.stat_ref = f32[32,8,128]{2,1,0:T(8,128)S(1)} all-to-all(f32[32,8,128]{2,1,0:T(8,128)S(1)} %get-tuple-element.83), channel_id=1, replica_groups=mesh['dp'=8,'rep'=4] {'dp','rep'}, dimensions={0} | all-to-all | bytes 262144 | tf_op jit(solution)/shard_map/all_to_all | solution.py:811
  54.8 4.3 %head.1 = (f32[47,1536]{1,0:T(8,128)}, f32[1,512]{1,0:T(1,128)S(1)}, f32[32,8,128]{2,1,0:T(8,128)S(1)}, f32[4,56,128]{2,1,0:T(8,128)S(1)}, f32[512,1536]{1,0:T(8,128)S(1)}, /*index=5*/f32[512,1536]{1,0:T(8,128)S(1)}) custom-call(f32[32,4,640]{2,1,0:T(4,128)S(1)} %all-to-all-done.pay_ref, f32[32,8,128]{2,1,0:T(8,128)S(1)} %all_to_all.25.stat_ref, ...), custom_call_target="tpu_custom_call" | custom-call | flops 2000000000 | bytes 10000000 | tf_op jit(solution)/shard_map/head/pallas_call | solution.py:813
  59.0 10.0 %all_to_all.26.sums_ref = f32[32,8,128]{2,1,0:T(8,128)S(1)} all-to-all(f32[32,8,128]{2,1,0:T(8,128)S(1)} %get-tuple-element.87), channel_id=1, replica_groups=mesh['dp'=8,'rep'=4] {'dp','rep'}, dimensions={0} | all-to-all | bytes 262144 | tf_op jit(solution)/shard_map/all_to_all | solution.py:831
  69.1 7.9 %mid_grad_send.1 = (f32[2,512,512]{2,1,0:T(8,128)S(1)}, f32[2,512]{1,0:T(2,128)S(1)}, bf16[1024,1536]{1,0:T(8,128)(2,1)S(1)}) custom-call(s32[2]{0:T(128)S(1)} %get-tuple-element.144.code_ref, f32[32,4,640]{2,1,0:T(4,128)S(1)} %all-to-all-done.pay_ref, f32[32,8,128]{2,1,0:T(8,128)S(1)} %all_to_all.26.sums_ref, f32[1,512]{1,0:T(1,128)S(1)} %get-tuple-element.88.inv_ref, ...), custom_call_target="tpu_custom_call" | custom-call | flops 4831838208 | bytes 10000000 | tf_op jit(solution)/shard_map/mid_grad_send/pallas_call | solution.py:834
  77.8 7.6 %mid_grad_keep.1 = f32[2,512,512]{2,1,0:T(8,128)S(1)} custom-call(s32[2]{0:T(128)S(1)} %get-tuple-element.144.code_ref, bf16[1024,1536]{1,0:T(8,128)(2,1)S(1)} %get-tuple-element.97.gcat.g, bf16[2,2048,1536]{2,1,0:T(8,128)(2,1)} %get-tuple-element.91.act_hbm), custom_call_target="tpu_custom_call" | custom-call | flops 4831838208 | bytes 10000000 | tf_op jit(solution)/shard_map/mid_grad_keep/pallas_call | solution.py:847
  87.3 26.6 %backward.1 = (f32[4,576,128]{2,1,0:T(8,128)S(1)}, f32[4,100,1536]{2,1,0:T(8,128)S(1)}) custom-call(s32[2]{0:T(128)S(1)} %get-tuple-element.145.code_ref, f32[32,4,640]{2,1,0:T(4,128)S(1)} %all-to-all-done.pay_ref, f32[4,1,512]{2,1,0:T(1,128)S(1)} %get-tuple-element.86.inv_ref, f32[4,1,512]{2,1,0:T(1,128)S(1)} %bitcast.47, ...), custom_call_target="tpu_custom_call" | custom-call | flops 12884901888 | bytes 24000000 | tf_op jit(solution)/shard_map/backward/pallas_call | solution.py:861
  114.3 2.0 %collective-permute-done.3 = f32[2,576,128]{2,1,0:T(8,128)S(1)} collective-permute-done((f32[2,576,128]{2,1,0:T(8,128)S(1)}, f32[2,576,128]{2,1,0:T(8,128)S(1)}, u32[]{:S(2)}, u32[]{:S(2)}) %collective-permute-start.3) | collective-permute-done | bytes 589856 | tf_op jit(solution)/shard_map/ppermute | solution.py:699
  120.1 3.5 %all-to-all-start.3 = ((f32[8,144,128]{2,1,0:T(8,128)}), f32[8,144,128]{2,1,0:T(8,128)S(1)}, u32[]{:S(2)}, u32[]{:S(2)}) async-start(f32[8,144,128]{2,1,0:T(8,128)} %bitcast.19), calls=%async_computation.3 | async-start | bytes 1179648 | tf_op jit(solution)/shard_map/all_to_all | solution.py:899
  123.7 2.0 collective-permute-done.4
  125.6 3.6 %collective-permute-done.5 = f32[128,512]{1,0:T(8,128)S(1)} collective-permute-done((f32[128,512]{1,0:T(8,128)S(1)}, f32[128,512]{1,0:T(8,128)S(1)}, u32[]{:S(2)}, u32[]{:S(2)}) %collective-permute-start.5) | collective-permute-done | bytes 262176 | tf_op jit(solution)/shard_map/ppermute | solution.py:699
  129.4 8.6 %collective-permute-done.6 = f32[2,2,32,512]{3,2,0,1:T(8,128)S(1)} collective-permute-done((f32[2,2,32,512]{3,2,0,1:T(8,128)S(1)}, f32[2,2,32,512]{3,2,0,1:T(8,128)S(1)}, u32[]{:S(2)}, u32[]{:S(2)}) %collective-permute-start.6) | collective-permute-done | bytes 262176 | tf_op jit(solution)/shard_map/ppermute | solution.py:699
  138.7 2.4 %collective-permute-start.8 = (f32[144,128]{1,0:T(8,128)S(1)}, f32[144,128]{1,0:T(8,128)S(1)}, u32[]{:S(2)}, u32[]{:S(2)}) collective-permute-start(f32[144,128]{1,0:T(8,128)S(1)} %reduce_sum.9), channel_id=1, source_target_pairs={{0,16},{1,17},{2,18},{3,19},{4,20},{5,21},{6,22},{7,23},{8,24},{9,... | collective-permute-start | bytes 221192 | tf_op jit(solution)/shard_map/ppermute | solution.py:699
  141.0 8.0 %collective-permute-done.8 = f32[144,128]{1,0:T(8,128)S(1)} collective-permute-done((f32[144,128]{1,0:T(8,128)S(1)}, f32[144,128]{1,0:T(8,128)S(1)}, u32[]{:S(2)}, u32[]{:S(2)}) %collective-permute-start.8) | collective-permute-done | bytes 73760 | tf_op jit(solution)/shard_map/ppermute | solution.py:699
  149.9 4.2 %all-to-all-start.4 = ((f32[8,144,128]{2,1,0:T(8,128)}), f32[8,144,128]{2,1,0:T(8,128)S(1)}, u32[]{:S(2)}, u32[]{:S(2)}) async-start(f32[8,144,128]{2,1,0:T(8,128)} %broadcast_in_dim.2), calls=%async_computation.4 | async-start | bytes 1179648 | tf_op jit(solution)/shard_map/all_to_all | solution.py:913
  154.1 2.1 %collective-permute-done.10 = f32[1,2,32,512]{3,2,0,1:T(8,128)S(1)} collective-permute-done((f32[1,2,32,512]{3,2,0,1:T(8,128)S(1)}, f32[1,2,32,512]{3,2,0,1:T(8,128)S(1)}, u32[]{:S(2)}, u32[]{:S(2)}) %collective-permute-start.10) | collective-permute-done | bytes 131104 | tf_op jit(solution)/shard_map/ppermute | solution.py:699
  156.4 11.8 %collective-permute-done.11 = f32[2,2,32,512]{3,2,0,1:T(8,128)S(1)} collective-permute-done((f32[2,2,32,512]{3,2,0,1:T(8,128)S(1)}, f32[2,2,32,512]{3,2,0,1:T(8,128)S(1)}, u32[]{:S(2)}, u32[]{:S(2)}) %collective-permute-start.11) | collective-permute-done | bytes 262176 | tf_op jit(solution)/shard_map/ppermute | solution.py:699
  171.3 3.6 %collective-permute-done.12 = f32[128,512]{1,0:T(8,128)S(1)} collective-permute-done((f32[128,512]{1,0:T(8,128)S(1)}, f32[128,512]{1,0:T(8,128)S(1)}, u32[]{:S(2)}, u32[]{:S(2)}) %collective-permute-start.12) | collective-permute-done | bytes 262176 | tf_op jit(solution)/shard_map/ppermute | solution.py:699
  179.8 9.1 %finish.1 = (f32[100,4,1536]{2,1,0:T(4,128)}, f32[100,4,512]{2,1,0:T(4,128)}, f32[4,1,512]{2,1,0:T(1,128)}, f32[4,1,512]{2,1,0:T(1,128)}, f32[4,1,512]{2,1,0:T(1...) custom-call(s32[2]{0:T(128)} %copy-done.8, ...), custom_call_target="tpu_custom_call" | custom-call | bytes 20000000 | tf_op jit(solution)/shard_map/finish/pallas_call | solution.py:930
  189.0 2.1 %place.3.refs_2_ = f32[2048,512]{1,0:T(8,128)} custom-call(s32[2]{0:T(128)S(1)} %get-tuple-element.144.code_ref, f32[256,512]{1,0:T(8,128)S(1)} %pad_maximum_fusion.refs_0_, f32[256,512]{1,0:T(8,128)S(1)} %pad_maximum_fusion.1.refs_1_, f32[256,512]{1,0:T(8,128)S(1)} %collective-permute-done.16.refs_2_, f32[256,512]{1,0:T(8,128)S(1)} %collective-permute-done.17.refs_3_), custom_call_target="tpu_custom_call" | custom-call | bytes 4000000 | tf_op jit(solution)/shard_map/place/pallas_call | solution.py:954
  (101 shorter events, 22.4 us)
Async XLA Ops:
  6.4 80.9 %copy-start.8 = (s32[2]{0:T(128)}, s32[2]{0:T(128)S(1)}, u32[]{:S(2)}) copy-start(s32[2]{0:T(128)S(1)} %get-tuple-element.145.code_ref) | copy-start | bytes 28
  6.5 19.3 %all-to-all-start = ((f32[32,4,640]{2,1,0:T(4,128)}), f32[32,4,640]{2,1,0:T(4,128)S(1)}, u32[]{:S(2)}, u32[]{:S(2)}) async-start(f32[32,4,640]{2,1,0:T(4,128)} %get-tuple-element.78), calls=%async_computation | async-start | bytes 655360 | tf_op jit(solution)/shard_map/all_to_all | solution.py:778
  77.6 7.9 %collective-permute-start = (f32[2,512,512]{2,1,0:T(8,128)S(1)}, f32[2,512,512]{2,1,0:T(8,128)S(1)}, u32[]{:S(2)}, u32[]{:S(2)}) collective-permute-start(f32[2,512,512]{2,1,0:T(8,128)S(1)} %get-tuple-element.93), channel_id=1, source_target_pairs={{0,1},{1,0},{2,3},{3,2},{4,5},{5,4},{6,7},{7,6},{8,9},{9,8},{10,11... | collective-permute-start | bytes 6291464 | tf_op jit(solution)/shard_map/ppermute | solution.py:699
  86.0 27.9 %collective-permute-start.1 = (f32[256,512]{1,0:T(8,128)S(1)}, f32[256,512]{1,0:T(8,128)S(1)}, u32[]{:S(2)}, u32[]{:S(2)}) collective-permute-start(f32[256,512]{1,0:T(8,128)S(1)} %slice_bitcast_fusion.2), channel_id=1, source_target_pairs={{0,2},{1,3},{2,0},{3,1},{4,6},{5,7},{6,4},{7,5},{8,10},{9,11},{10,... | collective-permute-start | bytes 1572872 | tf_op jit(solution)/shard_map/ppermute | solution.py:699
  86.5 27.6 %collective-permute-start.2 = (f32[256,512]{1,0:T(8,128)S(1)}, f32[256,512]{1,0:T(8,128)S(1)}, u32[]{:S(2)}, u32[]{:S(2)}) collective-permute-start(f32[256,512]{1,0:T(8,128)S(1)} %slice_bitcast_fusion.1), channel_id=1, source_target_pairs={{0,4},{1,5},{2,6},{3,7},{4,0},{5,1},{6,2},{7,3},{8,12},{9,13},{10,... | collective-permute-start | bytes 1572872 | tf_op jit(solution)/shard_map/ppermute | solution.py:699
  114.2 2.1 %collective-permute-start.3 = (f32[2,576,128]{2,1,0:T(8,128)S(1)}, f32[2,576,128]{2,1,0:T(8,128)S(1)}, u32[]{:S(2)}, u32[]{:S(2)}) collective-permute-start(f32[2,576,128]{2,1,0:T(8,128)S(1)} %slice.85), channel_id=1, source_target_pairs={{0,1},{1,0},{2,3},{3,2},{4,5},{5,4},{6,7},{7,6},{8,9},{9,8},{10,11... | collective-permute-start | bytes 1769480 | tf_op jit(solution)/shard_map/ppermute | solution.py:699
  117.2 8.4 %collective-permute-start.4 = (f32[128,512]{1,0:T(8,128)S(1)}, f32[128,512]{1,0:T(8,128)S(1)}, u32[]{:S(2)}, u32[]{:S(2)}) collective-permute-start(f32[128,512]{1,0:T(8,128)S(1)} %slice.87), channel_id=1, source_target_pairs={{0,4},{1,5},{2,6},{3,7},{4,0},{5,1},{6,2},{7,3},{8,12},{9,13},{10,... | collective-permute-start | bytes 786440 | tf_op jit(solution)/shard_map/ppermute | solution.py:699
  118.5 10.7 %collective-permute-start.5 = (f32[128,512]{1,0:T(8,128)S(1)}, f32[128,512]{1,0:T(8,128)S(1)}, u32[]{:S(2)}, u32[]{:S(2)}) collective-permute-start(f32[128,512]{1,0:T(8,128)S(1)} %slice.88), channel_id=1, source_target_pairs={{0,2},{1,3},{2,0},{3,1},{4,6},{5,7},{6,4},{7,5},{8,10},{9,11},{10,... | collective-permute-start | bytes 786440 | tf_op jit(solution)/shard_map/ppermute | solution.py:699
  120.1 17.9 %all-to-all-start.3 = ((f32[8,144,128]{2,1,0:T(8,128)}), f32[8,144,128]{2,1,0:T(8,128)S(1)}, u32[]{:S(2)}, u32[]{:S(2)}) async-start(f32[8,144,128]{2,1,0:T(8,128)} %bitcast.19), calls=%async_computation.3 | async-start | bytes 1179648 | tf_op jit(solution)/shard_map/all_to_all | solution.py:899
  129.3 8.6 %collective-permute-start.6 = (f32[2,2,32,512]{3,2,0,1:T(8,128)S(1)}, f32[2,2,32,512]{3,2,0,1:T(8,128)S(1)}, u32[]{:S(2)}, u32[]{:S(2)}) collective-permute-start(f32[2,2,32,512]{3,2,0,1:T(8,128)S(1)} %pad_maximum_fusion.2), channel_id=1, source_target_pairs={{0,8},{1,9},{2,10},{3,11},{4,12},{5,13},{6,14},{7,15},{8,0},{9,1},... | collective-permute-start | bytes 786440 | tf_op jit(solution)/shard_map/ppermute | solution.py:699
  138.0 11.0 %collective-permute-start.7 = (f32[1,2,32,512]{3,2,0,1:T(8,128)S(1)}, f32[1,2,32,512]{3,2,0,1:T(8,128)S(1)}, u32[]{:S(2)}, u32[]{:S(2)}) collective-permute-start(f32[1,2,32,512]{3,2,0,1:T(8,128)S(1)} %slice.92), channel_id=1, source_target_pairs={{0,16},{1,17},{2,18},{3,19},{4,20},{5,21},{6,22},{7,23},{8,24},{9,... | collective-permute-start | bytes 393224 | tf_op jit(solution)/shard_map/ppermute | solution.py:699
  138.7 10.4 %collective-permute-start.8 = (f32[144,128]{1,0:T(8,128)S(1)}, f32[144,128]{1,0:T(8,128)S(1)}, u32[]{:S(2)}, u32[]{:S(2)}) collective-permute-start(f32[144,128]{1,0:T(8,128)S(1)} %reduce_sum.9), channel_id=1, source_target_pairs={{0,16},{1,17},{2,18},{3,19},{4,20},{5,21},{6,22},{7,23},{8,24},{9,... | collective-permute-start | bytes 221192 | tf_op jit(solution)/shard_map/ppermute | solution.py:699
  149.9 6.3 %collective-permute-start.10 = (f32[1,2,32,512]{3,2,0,1:T(8,128)S(1)}, f32[1,2,32,512]{3,2,0,1:T(8,128)S(1)}, u32[]{:S(2)}, u32[]{:S(2)}) collective-permute-start(f32[1,2,32,512]{3,2,0,1:T(8,128)S(1)} %slice_add_fusion.5), channel_id=1, source_target_pairs={{0,16},{1,17},{2,18},{3,19},{4,20},{5,21},{6,22},{7,23},{8,24},{9,... | collective-permute-start | bytes 393224 | tf_op jit(solution)/shard_map/ppermute | solution.py:699
  149.9 26.3 %all-to-all-start.4 = ((f32[8,144,128]{2,1,0:T(8,128)}), f32[8,144,128]{2,1,0:T(8,128)S(1)}, u32[]{:S(2)}, u32[]{:S(2)}) async-start(f32[8,144,128]{2,1,0:T(8,128)} %broadcast_in_dim.2), calls=%async_computation.4 | async-start | bytes 1179648 | tf_op jit(solution)/shard_map/all_to_all | solution.py:913
  156.3 12.0 %collective-permute-start.11 = (f32[2,2,32,512]{3,2,0,1:T(8,128)S(1)}, f32[2,2,32,512]{3,2,0,1:T(8,128)S(1)}, u32[]{:S(2)}, u32[]{:S(2)}) collective-permute-start(f32[2,2,32,512]{3,2,0,1:T(8,128)S(1)} %pad_maximum_fusion.3), channel_id=1, source_target_pairs={{0,8},{1,9},{2,10},{3,11},{4,12},{5,13},{6,14},{7,15},{8,0},{9,1},... | collective-permute-start | bytes 786440 | tf_op jit(solution)/shard_map/ppermute | solution.py:699
  168.3 6.6 %collective-permute-start.12 = (f32[128,512]{1,0:T(8,128)S(1)}, f32[128,512]{1,0:T(8,128)S(1)}, u32[]{:S(2)}, u32[]{:S(2)}) collective-permute-start(f32[128,512]{1,0:T(8,128)S(1)} %bitcast.65), channel_id=1, source_target_pairs={{0,4},{1,5},{2,6},{3,7},{4,0},{5,1},{6,2},{7,3},{8,12},{9,13},{10,... | collective-permute-start | bytes 786440 | tf_op jit(solution)/shard_map/ppermute | solution.py:699
  169.8 6.4 %collective-permute-start.13 = (f32[128,512]{1,0:T(8,128)S(1)}, f32[128,512]{1,0:T(8,128)S(1)}, u32[]{:S(2)}, u32[]{:S(2)}) collective-permute-start(f32[128,512]{1,0:T(8,128)S(1)} %bitcast.63), channel_id=1, source_target_pairs={{0,2},{1,3},{2,0},{3,1},{4,6},{5,7},{6,4},{7,5},{8,10},{9,11},{10,... | collective-permute-start | bytes 786440 | tf_op jit(solution)/shard_map/ppermute | solution.py:699
  176.3 2.7 %collective-permute-start.9 = (f32[2,576,128]{2,1,0:T(8,128)S(1)}, f32[2,576,128]{2,1,0:T(8,128)S(1)}, u32[]{:S(2)}, u32[]{:S(2)}) collective-permute-start(f32[2,576,128]{2,1,0:T(8,128)S(1)} %bitcast.57), channel_id=1, source_target_pairs={{0,1},{1,0},{2,3},{3,2},{4,5},{5,4},{6,7},{7,6},{8,9},{9,8},{10,11... | collective-permute-start | bytes 1769480 | tf_op jit(solution)/shard_map/ppermute | solution.py:699
  176.4 12.6 %collective-permute-start.17 = (f32[256,512]{1,0:T(8,128)S(1)}, f32[256,512]{1,0:T(8,128)S(1)}, u32[]{:S(2)}, u32[]{:S(2)}) collective-permute-start(f32[256,512]{1,0:T(8,128)S(1)} %pad_maximum_fusion.1.refs_1_), channel_id=1, source_target_pairs={{0,1},{1,0},{2,3},{3,2},{4,5},{5,4},{6,7},{7,6},{8,9},{9,8},{10,11... | collective-permute-start | bytes 1572872 | tf_op jit(solution)/shard_map/ppermute | solution.py:699
  176.9 12.0 %collective-permute-start.16 = (f32[256,512]{1,0:T(8,128)S(1)}, f32[256,512]{1,0:T(8,128)S(1)}, u32[]{:S(2)}, u32[]{:S(2)}) collective-permute-start(f32[256,512]{1,0:T(8,128)S(1)} %pad_maximum_fusion.refs_0_), channel_id=1, source_target_pairs={{0,1},{1,0},{2,3},{3,2},{4,5},{5,4},{6,7},{7,6},{8,9},{9,8},{10,11... | collective-permute-start | bytes 1572872 | tf_op jit(solution)/shard_map/ppermute | solution.py:699
  177.0 14.3 %collective-permute-start.14 = (f32[256,512]{1,0:T(8,128)S(1)}, f32[256,512]{1,0:T(8,128)S(1)}, u32[]{:S(2)}, u32[]{:S(2)}) collective-permute-start(f32[256,512]{1,0:T(8,128)S(1)} %pad_maximum_fusion.refs_0_), channel_id=1, source_target_pairs={{0,2},{1,3},{2,0},{3,1},{4,6},{5,7},{6,4},{7,5},{8,10},{9,11},{10,... | collective-permute-start | bytes 1572872 | tf_op jit(solution)/shard_map/ppermute | solution.py:699
  178.5 14.0 %collective-permute-start.15 = (f32[256,512]{1,0:T(8,128)S(1)}, f32[256,512]{1,0:T(8,128)S(1)}, u32[]{:S(2)}, u32[]{:S(2)}) collective-permute-start(f32[256,512]{1,0:T(8,128)S(1)} %pad_maximum_fusion.1.refs_1_), channel_id=1, source_target_pairs={{0,4},{1,5},{2,6},{3,7},{4,0},{5,1},{6,2},{7,3},{8,12},{9,13},{10,... | collective-permute-start | bytes 1572872 | tf_op jit(solution)/shard_map/ppermute | solution.py:699
  192.5 2.2 %collective-permute-start.19 = (f32[256,512]{1,0:T(8,128)S(1)}, f32[256,512]{1,0:T(8,128)S(1)}, u32[]{:S(2)}, u32[]{:S(2)}) collective-permute-start(f32[256,512]{1,0:T(8,128)S(1)} %collective-permute-done.15.refs_1_), channel_id=1, source_target_pairs={{0,1},{1,0},{2,3},{3,2},{4,5},{5,4},{6,7},{7,6},{8,9},{9,8},{10,11... | collective-permute-start | bytes 1572872 | tf_op jit(solution)/shard_map/ppermute | solution.py:699
  192.5 2.7 %collective-permute-start.18 = (f32[256,512]{1,0:T(8,128)S(1)}, f32[256,512]{1,0:T(8,128)S(1)}, u32[]{:S(2)}, u32[]{:S(2)}) collective-permute-start(f32[256,512]{1,0:T(8,128)S(1)} %collective-permute-done.14.refs_0_), channel_id=1, source_target_pairs={{0,1},{1,0},{2,3},{3,2},{4,5},{5,4},{6,7},{7,6},{8,9},{9,8},{10,11... | collective-permute-start | bytes 1572872 | tf_op jit(solution)/shard_map/ppermute | solution.py:699
  (19 other events, 360.3 us)

commit v3 on v2

--- a/solution.py
+++ b/solution.py
@@ -571,12 +571,16 @@
         gram = gram_ref[h] + shift_col[h] * (own_shift * own_count)
         pack_ref[h ^ flip, at + HEAD_ROWS :, :] = gram[:HOP_ROWS]
 
-    def pack(h):
+    def slope_sums(h):
+        return total_row(acc[h % 2, 1]), 2.0 * total_row(acc[h % 2, 0])
+
+    def pack(h, sums=None):
         two = h % 2
+        slope1_sum, slope2_sum = sums or slope_sums(h)
         bias_sum = prod[two, feats : feats + 1, :]
         prod[two] = prod[two] + wide(shift_col[h], mid) * bias_sum
-        prod[two, feats + 1 : feats + 2, :] = total_row(acc[two, 1])
-        prod[two, feats + 2 : feats + 3, :] = 2.0 * total_row(acc[two, 0])
+        prod[two, feats + 1 : feats + 2, :] = slope1_sum
+        prod[two, feats + 2 : feats + 3, :] = slope2_sum
         for t in range(tiles):
             pack_ref[t ^ flip, h * HOP_ROWS : (h + 1) * HOP_ROWS, :] = prod[
                 two, :HOP_ROWS, t * LANES : (t + 1) * LANES
@@ -611,8 +615,9 @@
     for part in (0, 1):
         feature_product(len(stages) - 1, part)
     copies.send(feat.at[hops - 1], feat_hbm.at[hops - 1])
+    sums = slope_sums(hops - 1)
     weight_product(hops - 1)
-    pack(hops - 1)
+    pack(hops - 1, sums)
     copies.finish()
 
 

time: 200 us -> 200 us (level)
  no operation moved by 1% of the time
where the time goes in v3:
time: 200 us; the launch traced here: 197 us
  Pallas kernels  93.3 us (47%)
  waiting for transfers between devices  46.9 us (23%)
  starting transfers between devices  29 us (14%)
  blocking collectives  21.8 us (11%)
  local copies, waits for them, and re-layouts  2.61 us (1%)
    ppermute x20, waiting for transfers between devices, exchange(): lax.ppermute(values, axes, [(i, i ^ 1 << bit) for i in range(devices)])  44.8 us
    pallas_call x1, Pallas kernels, backward(): call(backward_kernel, 42, in_specs=[smem] + [vmem] * 9 + [anywhere] * 2,...  26.7 us
    pallas_call x1, Pallas kernels, on_device(): call(forward_kernel, 45, in_specs=[smem] + [vmem] * 7 + [anywhere] * 2, o...  17 us
    ppermute x20, starting transfers between devices, exchange(): lax.ppermute(values, axes, [(i, i ^ 1 << bit) for i in range(devices)])  13.8 us
    all_to_all x1, blocking collectives, on_device(): stat = gather(stat)  11.8 us
    all_to_all x1, blocking collectives, on_device(): sums = gather(sums)  10 us
    pallas_call x1, Pallas kernels, on_device(): call(prepare_kernel, 60, in_specs=[anywhere, vmem, anywhere], out_specs=[...  9.63 us
    pallas_call x1, Pallas kernels, on_device(): call(finish_kernel, 60, in_specs=[smem] + [vmem] * 8 + [anywhere] * 2, ou...  9.11 us
  transfers between devices with their start and end apart: 23, of which 13 were waited for; matrix products, arithmetic and copies ran while one was open for 0% of the time, Pallas kernels for 29%

profile of v3, /device:TPU:0, one launch (start us, length us, event | category | flops | bytes accessed | tf_op | source)
XLA Modules:
  0.0 197.1 jit_solution(11424606674284182822)
XLA Ops:
  0.7 5.7 %first_stats.1 = (f32[32,4,640]{2,1,0:T(4,128)}, f32[4,128,128]{2,1,0:T(8,128)}, bf16[4,256,1536]{2,1,0:T(8,128)(2,1)}, f32[4,100,512]{2,1,0:T(8,128)}) custom-call(f32[100,4,1536]{2,1,0:T(4,128)} %bitcast.67, f32[100,4,512]{2,1,0:T(4,128)} %bitcast.69, s32[1536]{0:T(1024)} %mask_ref.9), custom_call_target="tpu_custom_call" | custom-call | flops 1000000000 | bytes 8000000 | tf_op jit(solution)/shard_map/first_stats/pallas_call | solution.py:767
  6.5 7.5 %all-to-all-start = ((f32[32,4,640]{2,1,0:T(4,128)}), f32[32,4,640]{2,1,0:T(4,128)S(1)}, u32[]{:S(2)}, u32[]{:S(2)}) async-start(f32[32,4,640]{2,1,0:T(4,128)} %get-tuple-element.78), calls=%async_computation | async-start | bytes 655360 | tf_op jit(solution)/shard_map/all_to_all | solution.py:783
  14.0 9.6 %prepare.1 = (f32[2048,1536]{1,0:T(8,128)}, bf16[4,512,1024]{2,1,0:T(8,128)(2,1)}) custom-call(bf16[4,256,1536]{2,1,0:T(8,128)(2,1)} %get-tuple-element.80.xcat_hbm, f32[4,100,512]{2,1,0:T(8,128)} %get-tuple-element.79.w_ref, f32[2048,512]{1,0:T(8,128)} %w2.1), custom_call_target="tpu_custom_call" | custom-call | flops 12884901888 | bytes 20000000 | tf_op jit(solution)/shard_map/prepare/pallas_call | solution.py:785
  23.6 2.1 %all-to-all-done.pay_ref = f32[32,4,640]{2,1,0:T(4,128)S(1)} async-done(((f32[32,4,640]{2,1,0:T(4,128)}), f32[32,4,640]{2,1,0:T(4,128)S(1)}, u32[]{:S(2)}, u32[]{:S(2)}) %all-to-all-start) | async-done | bytes 327712 | tf_op jit(solution)/shard_map/all_to_all | solution.py:783
  25.9 17.0 %forward.1 = (f32[512,1536]{1,0:T(8,128)S(1)}, f32[32,8,128]{2,1,0:T(8,128)S(1)}, f32[4,1,512]{2,1,0:T(1,128)S(1)}, f32[4,512,128]{2,1,0:T(8,128)S(1)}, bf16[2,2048,1536]{2,1,0:T(8,128)(2,1)}) custom-call(s32[2]{0:T(128)S(1)} %get-tuple-element.145.code_ref, f32[32,4,640]{2,1,0:T(4,128)S(1)} %all-to-all-done.pay_ref, f32[4,100,512]{2,1,0:T(8,128)S(1)} %copy-done.2, ...), custom_call_target="tpu_custom_call" | custom-call | flops 9663676416 | bytes 20000000 | tf_op jit(solution)/shard_map/forward/pallas_call | solution.py:799
  42.9 11.8 %all_to_all.25.stat_ref = f32[32,8,128]{2,1,0:T(8,128)S(1)} all-to-all(f32[32,8,128]{2,1,0:T(8,128)S(1)} %get-tuple-element.83), channel_id=1, replica_groups=mesh['dp'=8,'rep'=4] {'dp','rep'}, dimensions={0} | all-to-all | bytes 262144 | tf_op jit(solution)/shard_map/all_to_all | solution.py:816
  54.8 4.3 %head.1 = (f32[47,1536]{1,0:T(8,128)}, f32[1,512]{1,0:T(1,128)S(1)}, f32[32,8,128]{2,1,0:T(8,128)S(1)}, f32[4,56,128]{2,1,0:T(8,128)S(1)}, f32[512,1536]{1,0:T(8,128)S(1)}, /*index=5*/f32[512,1536]{1,0:T(8,128)S(1)}) custom-call(f32[32,4,640]{2,1,0:T(4,128)S(1)} %all-to-all-done.pay_ref, f32[32,8,128]{2,1,0:T(8,128)S(1)} %all_to_all.25.stat_ref, ...), custom_call_target="tpu_custom_call" | custom-call | flops 2000000000 | bytes 10000000 | tf_op jit(solution)/shard_map/head/pallas_call | solution.py:818
  59.0 10.0 %all_to_all.26.sums_ref = f32[32,8,128]{2,1,0:T(8,128)S(1)} all-to-all(f32[32,8,128]{2,1,0:T(8,128)S(1)} %get-tuple-element.87), channel_id=1, replica_groups=mesh['dp'=8,'rep'=4] {'dp','rep'}, dimensions={0} | all-to-all | bytes 262144 | tf_op jit(solution)/shard_map/all_to_all | solution.py:836
  69.1 7.9 %mid_grad_send.1 = (f32[2,512,512]{2,1,0:T(8,128)S(1)}, f32[2,512]{1,0:T(2,128)S(1)}, bf16[1024,1536]{1,0:T(8,128)(2,1)S(1)}) custom-call(s32[2]{0:T(128)S(1)} %get-tuple-element.144.code_ref, f32[32,4,640]{2,1,0:T(4,128)S(1)} %all-to-all-done.pay_ref, f32[32,8,128]{2,1,0:T(8,128)S(1)} %all_to_all.26.sums_ref, f32[1,512]{1,0:T(1,128)S(1)} %get-tuple-element.88.inv_ref, ...), custom_call_target="tpu_custom_call" | custom-call | flops 4831838208 | bytes 10000000 | tf_op jit(solution)/shard_map/mid_grad_send/pallas_call | solution.py:839
  77.8 7.6 %mid_grad_keep.1 = f32[2,512,512]{2,1,0:T(8,128)S(1)} custom-call(s32[2]{0:T(128)S(1)} %get-tuple-element.144.code_ref, bf16[1024,1536]{1,0:T(8,128)(2,1)S(1)} %get-tuple-element.97.gcat.g, bf16[2,2048,1536]{2,1,0:T(8,128)(2,1)} %get-tuple-element.91.act_hbm), custom_call_target="tpu_custom_call" | custom-call | flops 4831838208 | bytes 10000000 | tf_op jit(solution)/shard_map/mid_grad_keep/pallas_call | solution.py:852
  87.3 26.7 %backward.1 = (f32[4,576,128]{2,1,0:T(8,128)S(1)}, f32[4,100,1536]{2,1,0:T(8,128)S(1)}) custom-call(s32[2]{0:T(128)S(1)} %get-tuple-element.145.code_ref, f32[32,4,640]{2,1,0:T(4,128)S(1)} %all-to-all-done.pay_ref, f32[4,1,512]{2,1,0:T(1,128)S(1)} %get-tuple-element.86.inv_ref, f32[4,1,512]{2,1,0:T(1,128)S(1)} %bitcast.47, ...), custom_call_target="tpu_custom_call" | custom-call | flops 12884901888 | bytes 24000000 | tf_op jit(solution)/shard_map/backward/pallas_call | solution.py:866
  114.3 2.0 %collective-permute-done.3 = f32[2,576,128]{2,1,0:T(8,128)S(1)} collective-permute-done((f32[2,576,128]{2,1,0:T(8,128)S(1)}, f32[2,576,128]{2,1,0:T(8,128)S(1)}, u32[]{:S(2)}, u32[]{:S(2)}) %collective-permute-start.3) | collective-permute-done | bytes 589856 | tf_op jit(solution)/shard_map/ppermute | solution.py:704
  120.1 3.5 %all-to-all-start.3 = ((f32[8,144,128]{2,1,0:T(8,128)}), f32[8,144,128]{2,1,0:T(8,128)S(1)}, u32[]{:S(2)}, u32[]{:S(2)}) async-start(f32[8,144,128]{2,1,0:T(8,128)} %bitcast.19), calls=%async_computation.3 | async-start | bytes 1179648 | tf_op jit(solution)/shard_map/all_to_all | solution.py:904
  123.7 2.0 collective-permute-done.4
  125.7 3.6 %collective-permute-done.5 = f32[128,512]{1,0:T(8,128)S(1)} collective-permute-done((f32[128,512]{1,0:T(8,128)S(1)}, f32[128,512]{1,0:T(8,128)S(1)}, u32[]{:S(2)}, u32[]{:S(2)}) %collective-permute-start.5) | collective-permute-done | bytes 262176 | tf_op jit(solution)/shard_map/ppermute | solution.py:704
  129.4 8.6 %collective-permute-done.6 = f32[2,2,32,512]{3,2,0,1:T(8,128)S(1)} collective-permute-done((f32[2,2,32,512]{3,2,0,1:T(8,128)S(1)}, f32[2,2,32,512]{3,2,0,1:T(8,128)S(1)}, u32[]{:S(2)}, u32[]{:S(2)}) %collective-permute-start.6) | collective-permute-done | bytes 262176 | tf_op jit(solution)/shard_map/ppermute | solution.py:704
  138.7 2.4 %collective-permute-start.8 = (f32[144,128]{1,0:T(8,128)S(1)}, f32[144,128]{1,0:T(8,128)S(1)}, u32[]{:S(2)}, u32[]{:S(2)}) collective-permute-start(f32[144,128]{1,0:T(8,128)S(1)} %reduce_sum.9), channel_id=1, source_target_pairs={{0,16},{1,17},{2,18},{3,19},{4,20},{5,21},{6,22},{7,23},{8,24},{9,... | collective-permute-start | bytes 221192 | tf_op jit(solution)/shard_map/ppermute | solution.py:704
  141.1 8.0 %collective-permute-done.8 = f32[144,128]{1,0:T(8,128)S(1)} collective-permute-done((f32[144,128]{1,0:T(8,128)S(1)}, f32[144,128]{1,0:T(8,128)S(1)}, u32[]{:S(2)}, u32[]{:S(2)}) %collective-permute-start.8) | collective-permute-done | bytes 73760 | tf_op jit(solution)/shard_map/ppermute | solution.py:704
  150.0 4.2 %all-to-all-start.4 = ((f32[8,144,128]{2,1,0:T(8,128)}), f32[8,144,128]{2,1,0:T(8,128)S(1)}, u32[]{:S(2)}, u32[]{:S(2)}) async-start(f32[8,144,128]{2,1,0:T(8,128)} %broadcast_in_dim.2), calls=%async_computation.4 | async-start | bytes 1179648 | tf_op jit(solution)/shard_map/all_to_all | solution.py:918
  154.2 2.1 %collective-permute-done.10 = f32[1,2,32,512]{3,2,0,1:T(8,128)S(1)} collective-permute-done((f32[1,2,32,512]{3,2,0,1:T(8,128)S(1)}, f32[1,2,32,512]{3,2,0,1:T(8,128)S(1)}, u32[]{:S(2)}, u32[]{:S(2)}) %collective-permute-start.10) | collective-permute-done | bytes 131104 | tf_op jit(solution)/shard_map/ppermute | solution.py:704
  156.4 11.8 %collective-permute-done.11 = f32[2,2,32,512]{3,2,0,1:T(8,128)S(1)} collective-permute-done((f32[2,2,32,512]{3,2,0,1:T(8,128)S(1)}, f32[2,2,32,512]{3,2,0,1:T(8,128)S(1)}, u32[]{:S(2)}, u32[]{:S(2)}) %collective-permute-start.11) | collective-permute-done | bytes 262176 | tf_op jit(solution)/shard_map/ppermute | solution.py:704
  171.3 3.6 %collective-permute-done.12 = f32[128,512]{1,0:T(8,128)S(1)} collective-permute-done((f32[128,512]{1,0:T(8,128)S(1)}, f32[128,512]{1,0:T(8,128)S(1)}, u32[]{:S(2)}, u32[]{:S(2)}) %collective-permute-start.12) | collective-permute-done | bytes 262176 | tf_op jit(solution)/shard_map/ppermute | solution.py:704
  179.9 9.1 %finish.1 = (f32[100,4,1536]{2,1,0:T(4,128)}, f32[100,4,512]{2,1,0:T(4,128)}, f32[4,1,512]{2,1,0:T(1,128)}, f32[4,1,512]{2,1,0:T(1,128)}, f32[4,1,512]{2,1,0:T(1...) custom-call(s32[2]{0:T(128)} %copy-done.8, ...), custom_call_target="tpu_custom_call" | custom-call | bytes 20000000 | tf_op jit(solution)/shard_map/finish/pallas_call | solution.py:935
  189.0 2.1 %place.3.refs_2_ = f32[2048,512]{1,0:T(8,128)} custom-call(s32[2]{0:T(128)S(1)} %get-tuple-element.144.code_ref, f32[256,512]{1,0:T(8,128)S(1)} %pad_maximum_fusion.refs_0_, f32[256,512]{1,0:T(8,128)S(1)} %pad_maximum_fusion.1.refs_1_, f32[256,512]{1,0:T(8,128)S(1)} %collective-permute-done.16.refs_2_, f32[256,512]{1,0:T(8,128)S(1)} %collective-permute-done.17.refs_3_), custom_call_target="tpu_custom_call" | custom-call | bytes 4000000 | tf_op jit(solution)/shard_map/place/pallas_call | solution.py:959
  (101 shorter events, 22.4 us)
Async XLA Ops:
  6.4 80.9 %copy-start.8 = (s32[2]{0:T(128)}, s32[2]{0:T(128)S(1)}, u32[]{:S(2)}) copy-start(s32[2]{0:T(128)S(1)} %get-tuple-element.145.code_ref) | copy-start | bytes 28
  6.5 19.3 %all-to-all-start = ((f32[32,4,640]{2,1,0:T(4,128)}), f32[32,4,640]{2,1,0:T(4,128)S(1)}, u32[]{:S(2)}, u32[]{:S(2)}) async-start(f32[32,4,640]{2,1,0:T(4,128)} %get-tuple-element.78), calls=%async_computation | async-start | bytes 655360 | tf_op jit(solution)/shard_map/all_to_all | solution.py:783
  77.6 7.9 %collective-permute-start = (f32[2,512,512]{2,1,0:T(8,128)S(1)}, f32[2,512,512]{2,1,0:T(8,128)S(1)}, u32[]{:S(2)}, u32[]{:S(2)}) collective-permute-start(f32[2,512,512]{2,1,0:T(8,128)S(1)} %get-tuple-element.93), channel_id=1, source_target_pairs={{0,1},{1,0},{2,3},{3,2},{4,5},{5,4},{6,7},{7,6},{8,9},{9,8},{10,11... | collective-permute-start | bytes 6291464 | tf_op jit(solution)/shard_map/ppermute | solution.py:704
  86.0 28.0 %collective-permute-start.1 = (f32[256,512]{1,0:T(8,128)S(1)}, f32[256,512]{1,0:T(8,128)S(1)}, u32[]{:S(2)}, u32[]{:S(2)}) collective-permute-start(f32[256,512]{1,0:T(8,128)S(1)} %slice_bitcast_fusion.2), channel_id=1, source_target_pairs={{0,2},{1,3},{2,0},{3,1},{4,6},{5,7},{6,4},{7,5},{8,10},{9,11},{10,... | collective-permute-start | bytes 1572872 | tf_op jit(solution)/shard_map/ppermute | solution.py:704
  86.5 27.6 %collective-permute-start.2 = (f32[256,512]{1,0:T(8,128)S(1)}, f32[256,512]{1,0:T(8,128)S(1)}, u32[]{:S(2)}, u32[]{:S(2)}) collective-permute-start(f32[256,512]{1,0:T(8,128)S(1)} %slice_bitcast_fusion.1), channel_id=1, source_target_pairs={{0,4},{1,5},{2,6},{3,7},{4,0},{5,1},{6,2},{7,3},{8,12},{9,13},{10,... | collective-permute-start | bytes 1572872 | tf_op jit(solution)/shard_map/ppermute | solution.py:704
  114.2 2.1 %collective-permute-start.3 = (f32[2,576,128]{2,1,0:T(8,128)S(1)}, f32[2,576,128]{2,1,0:T(8,128)S(1)}, u32[]{:S(2)}, u32[]{:S(2)}) collective-permute-start(f32[2,576,128]{2,1,0:T(8,128)S(1)} %slice.85), channel_id=1, source_target_pairs={{0,1},{1,0},{2,3},{3,2},{4,5},{5,4},{6,7},{7,6},{8,9},{9,8},{10,11... | collective-permute-start | bytes 1769480 | tf_op jit(solution)/shard_map/ppermute | solution.py:704
  117.3 8.4 %collective-permute-start.4 = (f32[128,512]{1,0:T(8,128)S(1)}, f32[128,512]{1,0:T(8,128)S(1)}, u32[]{:S(2)}, u32[]{:S(2)}) collective-permute-start(f32[128,512]{1,0:T(8,128)S(1)} %slice.87), channel_id=1, source_target_pairs={{0,4},{1,5},{2,6},{3,7},{4,0},{5,1},{6,2},{7,3},{8,12},{9,13},{10,... | collective-permute-start | bytes 786440 | tf_op jit(solution)/shard_map/ppermute | solution.py:704
  118.5 10.7 %collective-permute-start.5 = (f32[128,512]{1,0:T(8,128)S(1)}, f32[128,512]{1,0:T(8,128)S(1)}, u32[]{:S(2)}, u32[]{:S(2)}) collective-permute-start(f32[128,512]{1,0:T(8,128)S(1)} %slice.88), channel_id=1, source_target_pairs={{0,2},{1,3},{2,0},{3,1},{4,6},{5,7},{6,4},{7,5},{8,10},{9,11},{10,... | collective-permute-start | bytes 786440 | tf_op jit(solution)/shard_map/ppermute | solution.py:704
  120.1 17.9 %all-to-all-start.3 = ((f32[8,144,128]{2,1,0:T(8,128)}), f32[8,144,128]{2,1,0:T(8,128)S(1)}, u32[]{:S(2)}, u32[]{:S(2)}) async-start(f32[8,144,128]{2,1,0:T(8,128)} %bitcast.19), calls=%async_computation.3 | async-start | bytes 1179648 | tf_op jit(solution)/shard_map/all_to_all | solution.py:904
  129.3 8.6 %collective-permute-start.6 = (f32[2,2,32,512]{3,2,0,1:T(8,128)S(1)}, f32[2,2,32,512]{3,2,0,1:T(8,128)S(1)}, u32[]{:S(2)}, u32[]{:S(2)}) collective-permute-start(f32[2,2,32,512]{3,2,0,1:T(8,128)S(1)} %pad_maximum_fusion.2), channel_id=1, source_target_pairs={{0,8},{1,9},{2,10},{3,11},{4,12},{5,13},{6,14},{7,15},{8,0},{9,1},... | collective-permute-start | bytes 786440 | tf_op jit(solution)/shard_map/ppermute | solution.py:704
  138.1 11.0 %collective-permute-start.7 = (f32[1,2,32,512]{3,2,0,1:T(8,128)S(1)}, f32[1,2,32,512]{3,2,0,1:T(8,128)S(1)}, u32[]{:S(2)}, u32[]{:S(2)}) collective-permute-start(f32[1,2,32,512]{3,2,0,1:T(8,128)S(1)} %slice.92), channel_id=1, source_target_pairs={{0,16},{1,17},{2,18},{3,19},{4,20},{5,21},{6,22},{7,23},{8,24},{9,... | collective-permute-start | bytes 393224 | tf_op jit(solution)/shard_map/ppermute | solution.py:704
  138.7 10.4 %collective-permute-start.8 = (f32[144,128]{1,0:T(8,128)S(1)}, f32[144,128]{1,0:T(8,128)S(1)}, u32[]{:S(2)}, u32[]{:S(2)}) collective-permute-start(f32[144,128]{1,0:T(8,128)S(1)} %reduce_sum.9), channel_id=1, source_target_pairs={{0,16},{1,17},{2,18},{3,19},{4,20},{5,21},{6,22},{7,23},{8,24},{9,... | collective-permute-start | bytes 221192 | tf_op jit(solution)/shard_map/ppermute | solution.py:704
  150.0 6.3 %collective-permute-start.10 = (f32[1,2,32,512]{3,2,0,1:T(8,128)S(1)}, f32[1,2,32,512]{3,2,0,1:T(8,128)S(1)}, u32[]{:S(2)}, u32[]{:S(2)}) collective-permute-start(f32[1,2,32,512]{3,2,0,1:T(8,128)S(1)} %slice_add_fusion.5), channel_id=1, source_target_pairs={{0,16},{1,17},{2,18},{3,19},{4,20},{5,21},{6,22},{7,23},{8,24},{9,... | collective-permute-start | bytes 393224 | tf_op jit(solution)/shard_map/ppermute | solution.py:704
  150.0 26.3 %all-to-all-start.4 = ((f32[8,144,128]{2,1,0:T(8,128)}), f32[8,144,128]{2,1,0:T(8,128)S(1)}, u32[]{:S(2)}, u32[]{:S(2)}) async-start(f32[8,144,128]{2,1,0:T(8,128)} %broadcast_in_dim.2), calls=%async_computation.4 | async-start | bytes 1179648 | tf_op jit(solution)/shard_map/all_to_all | solution.py:918
  156.3 12.0 %collective-permute-start.11 = (f32[2,2,32,512]{3,2,0,1:T(8,128)S(1)}, f32[2,2,32,512]{3,2,0,1:T(8,128)S(1)}, u32[]{:S(2)}, u32[]{:S(2)}) collective-permute-start(f32[2,2,32,512]{3,2,0,1:T(8,128)S(1)} %pad_maximum_fusion.3), channel_id=1, source_target_pairs={{0,8},{1,9},{2,10},{3,11},{4,12},{5,13},{6,14},{7,15},{8,0},{9,1},... | collective-permute-start | bytes 786440 | tf_op jit(solution)/shard_map/ppermute | solution.py:704
  168.3 6.6 %collective-permute-start.12 = (f32[128,512]{1,0:T(8,128)S(1)}, f32[128,512]{1,0:T(8,128)S(1)}, u32[]{:S(2)}, u32[]{:S(2)}) collective-permute-start(f32[128,512]{1,0:T(8,128)S(1)} %bitcast.65), channel_id=1, source_target_pairs={{0,4},{1,5},{2,6},{3,7},{4,0},{5,1},{6,2},{7,3},{8,12},{9,13},{10,... | collective-permute-start | bytes 786440 | tf_op jit(solution)/shard_map/ppermute | solution.py:704
  169.9 6.4 %collective-permute-start.13 = (f32[128,512]{1,0:T(8,128)S(1)}, f32[128,512]{1,0:T(8,128)S(1)}, u32[]{:S(2)}, u32[]{:S(2)}) collective-permute-start(f32[128,512]{1,0:T(8,128)S(1)} %bitcast.63), channel_id=1, source_target_pairs={{0,2},{1,3},{2,0},{3,1},{4,6},{5,7},{6,4},{7,5},{8,10},{9,11},{10,... | collective-permute-start | bytes 786440 | tf_op jit(solution)/shard_map/ppermute | solution.py:704
  176.3 2.7 %collective-permute-start.9 = (f32[2,576,128]{2,1,0:T(8,128)S(1)}, f32[2,576,128]{2,1,0:T(8,128)S(1)}, u32[]{:S(2)}, u32[]{:S(2)}) collective-permute-start(f32[2,576,128]{2,1,0:T(8,128)S(1)} %bitcast.57), channel_id=1, source_target_pairs={{0,1},{1,0},{2,3},{3,2},{4,5},{5,4},{6,7},{7,6},{8,9},{9,8},{10,11... | collective-permute-start | bytes 1769480 | tf_op jit(solution)/shard_map/ppermute | solution.py:704
  176.4 12.6 %collective-permute-start.17 = (f32[256,512]{1,0:T(8,128)S(1)}, f32[256,512]{1,0:T(8,128)S(1)}, u32[]{:S(2)}, u32[]{:S(2)}) collective-permute-start(f32[256,512]{1,0:T(8,128)S(1)} %pad_maximum_fusion.1.refs_1_), channel_id=1, source_target_pairs={{0,1},{1,0},{2,3},{3,2},{4,5},{5,4},{6,7},{7,6},{8,9},{9,8},{10,11... | collective-permute-start | bytes 1572872 | tf_op jit(solution)/shard_map/ppermute | solution.py:704
  177.0 12.0 %collective-permute-start.16 = (f32[256,512]{1,0:T(8,128)S(1)}, f32[256,512]{1,0:T(8,128)S(1)}, u32[]{:S(2)}, u32[]{:S(2)}) collective-permute-start(f32[256,512]{1,0:T(8,128)S(1)} %pad_maximum_fusion.refs_0_), channel_id=1, source_target_pairs={{0,1},{1,0},{2,3},{3,2},{4,5},{5,4},{6,7},{7,6},{8,9},{9,8},{10,11... | collective-permute-start | bytes 1572872 | tf_op jit(solution)/shard_map/ppermute | solution.py:704
  177.1 14.3 %collective-permute-start.14 = (f32[256,512]{1,0:T(8,128)S(1)}, f32[256,512]{1,0:T(8,128)S(1)}, u32[]{:S(2)}, u32[]{:S(2)}) collective-permute-start(f32[256,512]{1,0:T(8,128)S(1)} %pad_maximum_fusion.refs_0_), channel_id=1, source_target_pairs={{0,2},{1,3},{2,0},{3,1},{4,6},{5,7},{6,4},{7,5},{8,10},{9,11},{10,... | collective-permute-start | bytes 1572872 | tf_op jit(solution)/shard_map/ppermute | solution.py:704
  178.5 14.0 %collective-permute-start.15 = (f32[256,512]{1,0:T(8,128)S(1)}, f32[256,512]{1,0:T(8,128)S(1)}, u32[]{:S(2)}, u32[]{:S(2)}) collective-permute-start(f32[256,512]{1,0:T(8,128)S(1)} %pad_maximum_fusion.1.refs_1_), channel_id=1, source_target_pairs={{0,4},{1,5},{2,6},{3,7},{4,0},{5,1},{6,2},{7,3},{8,12},{9,13},{10,... | collective-permute-start | bytes 1572872 | tf_op jit(solution)/shard_map/ppermute | solution.py:704
  192.5 2.2 %collective-permute-start.19 = (f32[256,512]{1,0:T(8,128)S(1)}, f32[256,512]{1,0:T(8,128)S(1)}, u32[]{:S(2)}, u32[]{:S(2)}) collective-permute-start(f32[256,512]{1,0:T(8,128)S(1)} %collective-permute-done.15.refs_1_), channel_id=1, source_target_pairs={{0,1},{1,0},{2,3},{3,2},{4,5},{5,4},{6,7},{7,6},{8,9},{9,8},{10,11... | collective-permute-start | bytes 1572872 | tf_op jit(solution)/shard_map/ppermute | solution.py:704
  192.5 2.7 %collective-permute-start.18 = (f32[256,512]{1,0:T(8,128)S(1)}, f32[256,512]{1,0:T(8,128)S(1)}, u32[]{:S(2)}, u32[]{:S(2)}) collective-permute-start(f32[256,512]{1,0:T(8,128)S(1)} %collective-permute-done.14.refs_0_), channel_id=1, source_target_pairs={{0,1},{1,0},{2,3},{3,2},{4,5},{5,4},{6,7},{7,6},{8,9},{9,8},{10,11... | collective-permute-start | bytes 1572872 | tf_op jit(solution)/shard_map/ppermute | solution.py:704
  (19 other events, 360.3 us)
